TPU v7x, 256 devices: a whole 4x4x8 slice. The times are simulated.
256 devices in a mesh: ctx: 64 (over z, y, core), tp: 4 (over x).
Axes of the slice: x: 4, y: 4, z: 8, core: 2. Of those that a mesh axis runs over, the one named last changes fastest.
Arguments:
- activations: bfloat16 [16384, 4096], P('ctx', 'tp'), may hold values from -0.875 to 0.875
- queries: bfloat16 [16384, 2048], P('ctx', 'tp'), may hold values from -7 to 7
- key_tensor: bfloat16 [16384, 512], P('ctx', 'tp'), may hold values from -4 to 4
- value_tensor: bfloat16 [16384, 512], P('ctx', 'tp'), may hold values from -6 to 6
- output_gradient: bfloat16 [16384, 2048], P('ctx', 'tp'), may hold values from -96 to 96
- selection: int32 [32, 3], replicated, may hold values from 0 to 30, as said below
- block_order: int32 [32], replicated, may hold values from 0 to 31, each once
Outputs:
- grad_queries: bfloat16 [16384, 2048], P('ctx', 'tp')
- key_gradient: bfloat16 [16384, 512], P('ctx', 'tp')
- value_gradient: bfloat16 [16384, 512], P('ctx', 'tp')
- grad_key_weight: float32 [4096, 512], P('ctx', 'tp')
- grad_value_weight: float32 [4096, 512], P('ctx', 'tp')
Inputs may be any that keep to these rules, and one draw needn't show every extreme that they name: `selection`: row b holds entries of 0 to b; its entries below b are distinct, and an entry equal to b marks an empty slot, which occurs only in rows b < 3. The last row selects block 30. Stored block s, rows s * 512 to (s + 1) * 512 - 1 of every token array, holds sequence block block_order[s].
All inputs are finite; a program needn't handle non-finite values.
Results may differ from a plain program's by a relative error of at most 0.0089.
Values may be sent and summed in bfloat16 or wider, within the bound.
A program may use at most 128 MiB of HBM per device.

v0:
```python
import jax
import jax.numpy as jnp
from jax import lax
from jax.sharding import PartitionSpec as P

HEAD_SIZE = 128
BLOCK_TOKENS = 512
PICKED_BLOCKS = 3


NEG_FILL = -1e30


def block_scores(query_rows, key_lines, scale_value, allowed):
    scores = (
        jnp.einsum("rgpd,lgd->gprl", query_rows, key_lines, preferred_element_type=jnp.float32)
        * scale_value
    )
    return jnp.where(allowed[None, None], scores, NEG_FILL)


def window_from(padded, start, margin, length):
    limit = padded.shape[0] - length
    return lax.dynamic_slice_in_dim(padded, jnp.clip(start + margin, 0, limit), length, 0)


def body(activations, queries, key_tensor, value_tensor, output_gradient, selection, block_order):
    row_count = queries.shape[0]
    kv_width = key_tensor.shape[1]
    group_count = kv_width // HEAD_SIZE
    query_heads_each = queries.shape[1] // kv_width
    position = lax.axis_index("ctx")
    parity = position % 2
    block_total = block_order.shape[0]
    selected = PICKED_BLOCKS + 1
    inverse = (
        jnp.zeros((block_total,), jnp.int32)
        .at[block_order]
        .set(jnp.arange(block_total, dtype=jnp.int32))
    )
    own_block = block_order[position // 2]
    listed = selection[own_block]
    chosen = jnp.concatenate([listed, own_block[None]])
    active = jnp.concatenate([listed != own_block, jnp.ones((1,), jnp.bool_)])
    starts = inverse[chosen] * BLOCK_TOKENS

    def collect(carried, pieces):
        piece_rows = pieces[0].shape[0]
        edge = jnp.zeros((BLOCK_TOKENS, kv_width), pieces[0].dtype)
        padded_keys = jnp.concatenate([edge, pieces[0], edge], axis=0)
        padded_values = jnp.concatenate([edge, pieces[1], edge], axis=0)
        key_acc, value_acc = carried
        for block_number in range(selected):
            shift_rows = starts[block_number]
            intersection = (shift_rows < piece_rows) & (shift_rows + BLOCK_TOKENS > 0)

            def place(accs, shift_rows=shift_rows, block_number=block_number):
                key_portion = window_from(padded_keys, shift_rows, BLOCK_TOKENS, BLOCK_TOKENS)
                value_portion = window_from(padded_values, shift_rows, BLOCK_TOKENS, BLOCK_TOKENS)
                row_start = block_number * BLOCK_TOKENS
                old_key = lax.dynamic_slice_in_dim(accs[0], row_start, BLOCK_TOKENS, 0)
                old_value = lax.dynamic_slice_in_dim(accs[1], row_start, BLOCK_TOKENS, 0)
                return (
                    lax.dynamic_update_slice_in_dim(accs[0], old_key + key_portion, row_start, 0),
                    lax.dynamic_update_slice_in_dim(
                        accs[1], old_value + value_portion, row_start, 0
                    ),
                )

            key_acc, value_acc = lax.cond(
                intersection, place, lambda accs: accs, (key_acc, value_acc)
            )
        return (key_acc, value_acc)

    blank_rows = jnp.zeros((selected * BLOCK_TOKENS, kv_width), key_tensor.dtype)
    key_chosen, value_chosen = collect(
        (blank_rows, blank_rows),
        (
            lax.all_gather(key_tensor, "ctx", axis=0, tiled=True),
            lax.all_gather(value_tensor, "ctx", axis=0, tiled=True),
        ),
    )
    scale_value = HEAD_SIZE ** (-0.5)
    query_rows = queries.reshape(row_count, group_count, query_heads_each, HEAD_SIZE)
    grad_rows = output_gradient.reshape(row_count, group_count, query_heads_each, HEAD_SIZE)
    query_offset = parity * row_count + jnp.arange(row_count)
    key_offset = jnp.arange(BLOCK_TOKENS)
    causal = key_offset[None, :] <= query_offset[:, None]

    def allowed_for(block_number):
        if block_number == PICKED_BLOCKS:
            return causal
        return jnp.broadcast_to(active[block_number], causal.shape)

    def block_rows(source, block_number):
        return source[block_number * BLOCK_TOKENS : (block_number + 1) * BLOCK_TOKENS].reshape(
            BLOCK_TOKENS, group_count, HEAD_SIZE
        )

    running_max = jnp.full((group_count, query_heads_each, row_count), NEG_FILL, jnp.float32)
    running_sum = jnp.zeros((group_count, query_heads_each, row_count), jnp.float32)
    visit_order = [PICKED_BLOCKS] + list(range(PICKED_BLOCKS))
    for block_number in visit_order:
        scores = block_scores(
            query_rows, block_rows(key_chosen, block_number), scale_value, allowed_for(block_number)
        )
        new_max = jnp.maximum(running_max, jnp.max(scores, axis=-1))
        running_sum = running_sum * jnp.exp(running_max - new_max) + jnp.sum(
            jnp.exp(scores - new_max[..., None]), axis=-1
        )
        running_max = new_max
    weight_blocks = []
    output_acc = jnp.zeros((row_count, group_count, query_heads_each, HEAD_SIZE), jnp.float32)
    for block_number in range(selected):
        scores = block_scores(
            query_rows, block_rows(key_chosen, block_number), scale_value, allowed_for(block_number)
        )
        weights = jnp.exp(scores - running_max[..., None]) / running_sum[..., None]
        weight_blocks.append(weights)
        weights_low = weights.astype(jnp.bfloat16)
        output_acc = output_acc + jnp.einsum(
            "gprl,lgd->rgpd",
            weights_low,
            block_rows(value_chosen, block_number),
            preferred_element_type=jnp.float32,
        )
    row_delta = jnp.sum(grad_rows.astype(jnp.float32) * output_acc, axis=-1).transpose(1, 2, 0)
    query_grad = jnp.zeros((row_count, group_count, query_heads_each, HEAD_SIZE), jnp.float32)
    key_portions = []
    value_portions = []
    for block_number in range(selected):
        weights = weight_blocks[block_number]
        weights_low = weights.astype(jnp.bfloat16)
        key_lines = block_rows(key_chosen, block_number)
        value_lines = block_rows(value_chosen, block_number)
        grad_probs = jnp.einsum(
            "rgpd,lgd->gprl", grad_rows, value_lines, preferred_element_type=jnp.float32
        )
        grad_scores = (weights * (grad_probs - row_delta[..., None])).astype(jnp.bfloat16)
        query_grad = query_grad + jnp.einsum(
            "gprl,lgd->rgpd", grad_scores, key_lines, preferred_element_type=jnp.float32
        )
        key_portions.append(
            jnp.einsum(
                "gprl,rgpd->lgd", grad_scores, query_rows, preferred_element_type=jnp.float32
            ).reshape(BLOCK_TOKENS, kv_width)
            * scale_value
        )
        value_portions.append(
            jnp.einsum(
                "gprl,rgpd->lgd", weights_low, grad_rows, preferred_element_type=jnp.float32
            ).reshape(BLOCK_TOKENS, kv_width)
        )
    grad_queries = (query_grad * scale_value).astype(jnp.bfloat16).reshape(row_count, -1)
    both_blocks = [
        jnp.concatenate([key_portions[block_number], value_portions[block_number]], axis=1)
        for block_number in range(selected)
    ]
    term_rows = lax.axis_size("ctx") * row_count
    accumulated = jnp.zeros((term_rows + 2 * BLOCK_TOKENS, 2 * kv_width), jnp.float32)
    for block_number in range(selected):
        shift_rows = starts[block_number]
        intersection = (shift_rows < term_rows) & (shift_rows + BLOCK_TOKENS > 0)

        def add_block(total, shift_rows=shift_rows, block_number=block_number):
            place_at = jnp.clip(shift_rows + BLOCK_TOKENS, 0, term_rows + BLOCK_TOKENS)
            old_rows = lax.dynamic_slice_in_dim(total, place_at, BLOCK_TOKENS, 0)
            return lax.dynamic_update_slice_in_dim(
                total, old_rows + both_blocks[block_number], place_at, 0
            )

        accumulated = lax.cond(intersection, add_block, lambda total: total, accumulated)
    returned = lax.psum_scatter(
        accumulated[BLOCK_TOKENS : BLOCK_TOKENS + term_rows], "ctx", scatter_dimension=0, tiled=True
    )
    key_grand_sum = returned[:, :kv_width]
    value_grand_sum = returned[:, kv_width:]
    key_gradient = key_grand_sum.astype(jnp.bfloat16)
    value_gradient = value_grand_sum.astype(jnp.bfloat16)
    full_features = lax.all_gather(activations, "tp", axis=1, tiled=True)
    both_grads = jnp.concatenate([key_gradient, value_gradient], axis=1)
    weight_sum = lax.psum_scatter(
        lax.dot_general(
            full_features, both_grads, (((0,), (0,)), ((), ())), preferred_element_type=jnp.float32
        ),
        "ctx",
        scatter_dimension=0,
        tiled=True,
    )
    return (
        grad_queries,
        key_gradient,
        value_gradient,
        weight_sum[:, :kv_width],
        weight_sum[:, kv_width:],
    )


def solution(mesh):
    placed = (
        P("ctx", "tp"),
        P("ctx", "tp"),
        P("ctx", "tp"),
        P("ctx", "tp"),
        P("ctx", "tp"),
        P(),
        P(),
    )
    return jax.shard_map(
        body,
        mesh=mesh,
        in_specs=placed,
        out_specs=(P("ctx", "tp"), P("ctx", "tp"), P("ctx", "tp"), P("ctx", "tp"), P("ctx", "tp")),
        check_vma=False,
    )
```

profile of v0, /device:TPU:1, one launch (start us, length us, event | category | flops | bytes accessed | tf_op | source)
XLA Modules:
  0.0 602.8 jit_solution(4818147939202217674)
XLA Ops:
  8.1 0.7 all-gather.4.cloned.1.call-update
  8.8 0.7 all-gather.6.cloned.1.call-update
  9.6 1.2 dynamic_slice.61
  12.8 0.9 dynamic-slice_reduce_fusion
  13.6 0.7 compare_select_fusion.1
  14.3 0.7 scatter_custom_fusion
  15.0 0.7 fusion.73
  15.7 0.6 gather_fusion
  16.3 0.6 fusion.86
  21.9 1.8 copy.199
  23.7 1.9 copy.117
  25.8 0.7 dynamic-slice_compare_fusion
  27.0 0.7 iota_compare_fusion
  27.8 67.1 %all-gather.4.cloned.1.call-done = bf16[16384,128]{1,0:T(8,128)(2,1)} async-done(((bf16[256,128]{1,0:T(8,128)(2,1)}), bf16[16384,128]{1,0:T(8,128)(2,1)}) %all-gather.4.cloned.1.call-update) | async-done | bytes 4194320 | tf_op jit(solution)/shard_map/all_gather | solution.py:79
  94.9 79.1 %all-gather.6.cloned.1.call-done = bf16[16384,128]{1,0:T(8,128)(2,1)} async-done(((bf16[256,128]{1,0:T(8,128)(2,1)}), bf16[16384,128]{1,0:T(8,128)(2,1)}) %all-gather.6.cloned.1.call-update) | async-done | bytes 4194320 | tf_op jit(solution)/shard_map/all_gather | solution.py:80
  174.0 13.6 %pad_maximum_fusion = (bf16[17408,128]{1,0:T(8,128)(2,1)}, bf16[17408,128]{1,0:T(8,128)(2,1)}) fusion(bf16[512,128]{1,0:T(8,128)(2,1)S(1)} %broadcast_in_dim.92, bf16[16384,128]{1,0:T(8,128)(2,1)} %all-gather.6.cloned.1.call-done, bf16[16384,128]{1,0:T(8,128)(2,1)} %all-gather.4.cloned.1.call-done), kind=kLoop, calls=%fused_computation.13 | loop fusion | flops 22282240 | bytes 17432576 | tf_op jit(solution)/shard_map/concatenate | solution.py:51
  187.7 1.8 conditional.8
  188.3 1.0 constant_dynamic-slice_fusion
  189.5 1.8 conditional.9
  190.2 1.1 add_dynamic-update-slice_fusion
  191.3 1.8 conditional.10
  192.0 1.1 add_dynamic-update-slice_fusion.2
  193.1 1.8 conditional.11
  193.7 1.1 dynamic-slice_add_fusion
  195.0 1.1 bitcast_reduce_fusion.2
  196.1 1.1 bitcast_reduce_fusion.1
  197.2 1.1 bitcast_reduce_fusion
  198.8 1.4 exponential_reduce_fusion
  201.1 2.0 convolution_bitcast_fusion.3
  203.1 1.2 convolution_bitcast_fusion.7
  204.4 1.2 convolution_bitcast_fusion.5
  205.6 1.0 copy.120
  206.6 2.1 fusion.39
  209.1 1.2 copy-done.1
  210.9 1.1 copy-done.5
  212.0 1.4 convolution_add_fusion.4
  213.4 1.2 convolution_bitcast_fusion.1
  216.2 1.3 fusion.21
  219.1 1.2 fusion.28
  220.9 10.3 %conditional.12 = (f32[17408,256]{1,0:T(8,128)}) conditional(s32[]{:T(128)} %convert_element_type.64, () %tuple.75, (s32[]{:T(128)}, f32[512,256]{0,1:T(8,128)S(1)}) %tuple.76), branch_computations={%region_18.19_spmd, %region_19.20_spmd} | conditional | flops 3 | bytes 19922996 | solution.py:172
  221.8 6.4 %broadcast_in_dim.80 = f32[17408,256]{1,0:T(8,128)} broadcast(f32[]{:T(128)} %constant.64.clone), dimensions={} | broadcast | bytes 17825796 | tf_op jit(solution)/shard_map/broadcast_in_dim | solution.py:160
  228.2 2.9 dynamic_update_slice.30
  231.2 5.0 conditional.13
  232.0 1.1 dynamic-slice_add_fusion.2
  233.2 3.0 dynamic_update_slice.31
  236.1 1.0 pad_maximum_fusion.6
  237.1 5.0 conditional.14
  238.0 1.1 dynamic-slice_add_fusion.3
  239.2 3.0 dynamic_update_slice.32
  242.1 1.0 pad_maximum_fusion.7
  243.1 5.1 conditional.15
  244.1 1.1 dynamic-slice_add_fusion.4
  245.3 3.0 dynamic_update_slice.33
  248.2 11.3 %slice.145 = f32[16384,256]{1,0:T(8,128)} slice(f32[17408,256]{1,0:T(8,128)} %get-tuple-element.288), slice={[512:16896], [0:256]} | slice | bytes 33554432 | tf_op jit(solution)/shard_map/slice | solution.py:174
  260.2 181.6 %reduce-scatter.5.cloned.1.call-done = f32[256,256]{1,0:T(8,128)} async-done(((f32[16384,256]{1,0:T(8,128)}), f32[256,256]{1,0:T(8,128)}) %reduce-scatter.5.cloned.1.call-update) | async-done | bytes 262160 | tf_op jit(solution)/shard_map/reduce_scatter | solution.py:173
  441.7 1.0 convert.9
  442.7 4.3 convolution_bitcast_fusion
  447.1 5.6 copy.194
  452.7 1.2 copy-done.9
  454.2 0.9 copy-done.11
  456.7 0.8 copy.159
  457.5 0.7 fusion.83
  458.2 136.1 %reduce-scatter.7.cloned.1.call-done = f32[64,256]{1,0:T(8,128)} async-done(((f32[4096,256]{1,0:T(8,128)}), f32[64,256]{1,0:T(8,128)}) %reduce-scatter.7.cloned.1.call-update) | async-done | bytes 65552
  594.3 1.4 fusion.84
  (85 shorter events, 10.3 us)
Async XLA Ops:
  8.0 17.8 %copy-start.23 = (s32[32,3]{0,1:T(4,128)S(1)}, s32[32,3]{0,1:T(4,128)}, u32[]{:S(2)}) copy-start(s32[32,3]{0,1:T(4,128)} %param.28) | copy-start | bytes 1156
  8.0 17.6 %copy-start.20 = (bf16[256,512]{1,0:T(8,128)(2,1)S(1)}, bf16[256,512]{1,0:T(8,128)(2,1)}, u32[]{:S(2)}) copy-start(bf16[256,512]{1,0:T(8,128)(2,1)} %param.24) | copy-start | bytes 786436
  8.0 86.9 %all-gather.4.cloned.1.call-start = ((), (), s32[]{:S(2)}) async-start(), calls=%async_computation.2 | async-start | bytes 4259840 | tf_op jit(solution)/shard_map/all_gather | solution.py:79
  8.8 165.3 %all-gather.6.cloned.1.call-start = ((), (), s32[]{:S(2)}) async-start(), calls=%async_computation.3 | async-start | bytes 4259840 | tf_op jit(solution)/shard_map/all_gather | solution.py:80
  9.5 432.2 %reduce-scatter.5.cloned.1.call-start = ((), (), s32[]{:S(2)}) async-start(), calls=%async_computation.4 | async-start | bytes 17039360 | tf_op jit(solution)/shard_map/reduce_scatter | solution.py:173
  195.0 2.2 copy-start.17
  196.1 7.1 %copy-start.2 = (f32[512,256,4]{1,0,2:T(8,128)}, f32[512,256,4]{1,0,2:T(8,128)S(1)}, u32[]{:S(2)}) copy-start(f32[512,256,4]{1,0,2:T(8,128)S(1)} %get-tuple-element.256) | copy-start | bytes 6291460
  196.1 2.2 copy-start.16
  197.2 7.2 %copy-start = (f32[512,256,4]{1,0,2:T(8,128)}, f32[512,256,4]{1,0,2:T(8,128)S(1)}, u32[]{:S(2)}) copy-start(f32[512,256,4]{1,0,2:T(8,128)S(1)} %get-tuple-element.254) | copy-start | bytes 6291460
  198.3 2.5 copy-start.4
  200.2 1.0 copy-start.13
  208.7 1.6 copy-start.1
  208.8 1.7 copy-start.19
  210.4 1.6 copy-start.5
  212.0 1.4 copy-start.14
  212.0 2.6 copy-start.12
  212.0 2.6 copy-start.18
  213.4 1.7 copy-start.3
  215.7 4.7 copy-start.8
  216.2 2.9 copy-start.6
  218.2 2.2 copy-start.10
  218.6 2.2 copy-start.22
  219.1 1.7 copy-start.21
  237.1 5.0 copy-start.15
  259.5 183.2 %all-gather.8.cloned.1.call-start = ((), (), s32[]{:S(2)}) async-start(), calls=%async_computation.5 | async-start | bytes 2621440 | tf_op jit(solution)/shard_map/all_gather | solution.py:180
  260.1 334.2 %reduce-scatter.7.cloned.1.call-start = ((), (), s32[]{:S(2)}) async-start(), calls=%async_computation.6 | async-start | bytes 4259840
  452.7 1.2 copy-start.9
  453.9 1.2 copy-start.11
  455.1 1.2 copy-start.7
Sparse Core Ops, SparseCore 0:
  11.6 83.2 all-gather.3
  97.7 76.2 all-gather.5
  259.7 182.0 reduce-scatter.4
  452.8 141.4 reduce-scatter.6
Sparse Core Ops, SparseCore 1:
  261.8 29.9 all-gather.7
where the time goes:
time: 609 us; the launch traced here: 603 us
  waiting for transfers between devices  466 us (77%)
  local copies, waits for them, and re-layouts  55.1 us (9%)
  other arithmetic  28.5 us (5%)
  matrix products  25 us (4%)
  between operations  22.6 us (4%)
    reduce_scatter x1, waiting for transfers between devices, body(): lax.psum_scatter(accumulated[BLOCK_TOKENS:BLOCK_TOKENS + term_rows], 'ctx...  182 us
    unnamed x6, waiting for transfers between devices  138 us
    all_gather x1, waiting for transfers between devices, body(): lax.all_gather(value_tensor, 'ctx', axis=0, tiled=True)  79.1 us
    all_gather x1, waiting for transfers between devices, body(): lax.all_gather(key_tensor, 'ctx', axis=0, tiled=True)  67.1 us
    concatenate x1, other arithmetic, collect(): padded_values = jnp.concatenate([edge, pieces[1], edge], axis=0)  13.6 us
  transfers between devices with their start and end apart: 5, of which 4 were waited for; matrix products, arithmetic and copies ran while one was open for 2% of the time, Pallas kernels for 0%

commit v1 on v0

v1 whole, which is shorter than its diff:
```python
import functools
import math

import jax
import jax.numpy as jnp
from jax import lax
from jax.experimental import pallas as pl
from jax.experimental.pallas import tpu as pltpu
from jax.sharding import PartitionSpec as P

MESH = pl.DeviceIdType.MESH
F32 = jnp.float32
BF16 = jnp.bfloat16

HEAD = 128
BLOCK = 512
HALF = 256
PICKS = 3
CHIPS = 32
ROWS_Y = 4
ROWS_Z = 8
ROWS_X = 4
PIECE = BLOCK // CHIPS
HEADS = 4
QUERIES = HEADS * HALF
SCALE = HEAD**-0.5
EXP_SCALE = SCALE * math.log2(math.e)
LOW = -1e30
HIGH = 1e30

(LOAD, P1, OWN, ACT1, P2, SWAP, ACT3, BACK2, BACK1, HALVES, GATHER, SUMS, LAST) = range(13)
BACK0 = 13
ALONG_X = BACK0 + PICKS + 1
SEMS = ALONG_X + ROWS_X


def rows_dot(left, right):
    return lax.dot_general(left, right, (((1,), (1,)), ((), ())), preferred_element_type=F32)


def plain_dot(left, right):
    return lax.dot_general(left, right, (((1,), (0,)), ((), ())), preferred_element_type=F32)


def kernel(
    table,
    live,
    columns,
    act_in,
    q_in,
    k_in,
    v_in,
    go_in,
    dq_out,
    dkv_out,
    dw_out,
    qd,
    own,
    held,
    picked,
    kv,
    key_t,
    scores,
    gprobs,
    low,
    cross,
    crossed,
    terms,
    landed,
    member,
    sums,
    final,
    own_terms,
    grads,
    all_grads,
    grads_t,
    acts,
    wide,
    wide_in,
    w_send,
    w_rows,
    send,
    recv,
):
    c = lax.axis_index("ctx")
    x = lax.axis_index("tp")
    chip = c // 2
    core = c % 2
    z = chip // ROWS_Y
    y = chip % ROWS_Y
    other = 1 - core
    sibling = c + 1 - 2 * core

    def remote(src, dst, sem, ctx, tp=None):
        return pltpu.make_async_remote_copy(
            src_ref=src,
            dst_ref=dst,
            send_sem=send.at[sem],
            recv_sem=recv.at[sem],
            device_id=(ctx, x if tp is None else tp),
            device_id_type=MESH,
        )

    def local(src, dst, sem):
        return pltpu.make_async_copy(src, dst, recv.at[sem])

    def arrived(ref, sem):
        pltpu.make_async_copy(ref, ref, recv.at[sem]).wait()

    def sent(ref, sem):
        pltpu.make_async_copy(ref, ref, send.at[sem]).wait()

    barrier = pltpu.get_barrier_semaphore()

    def greet(d, carry):
        pl.semaphore_signal(
            barrier, inc=1, device_id=(lax.rem(c + d, 2 * CHIPS), x), device_id_type=MESH
        )
        return carry

    lax.fori_loop(1, 2 * CHIPS, greet, 0)
    for d in range(1, ROWS_X):
        pl.semaphore_signal(
            barrier, inc=1, device_id=(c, lax.rem(x + d, ROWS_X)), device_id_type=MESH
        )

    for h in range(HEADS):
        strip = pl.ds(h * HEAD, HEAD)
        block = pl.ds(h * HALF, HALF)
        local(q_in.at[:, strip], qd.at[0, block], LOAD).start()
        local(go_in.at[:, strip], qd.at[1, block], LOAD).start()

    pl.semaphore_wait(barrier, 2 * CHIPS - 1 + ROWS_X - 1)

    def spread(j, carry):
        rows = pl.ds(pl.multiple_of(j * PIECE, PIECE), PIECE)
        for kind, src in ((0, k_in), (1, v_in)):
            target = (core * (CHIPS // 2) + j) * 2 + kind

            @pl.when(target != c)
            def _():
                remote(src.at[rows], held.at[chip], P1, target).start()

            @pl.when(target == c)
            def _():
                local(src.at[rows], held.at[chip], P1).start()

        return carry

    lax.fori_loop(0, CHIPS // 2, spread, 0)

    my_rows = pl.ds(pl.multiple_of(core * HALF, HALF), HALF)
    for kind, src in ((0, k_in), (1, v_in)):
        remote(src, own.at[kind, my_rows], OWN, sibling).start()
        local(src, own.at[kind, my_rows], OWN).start()

    for d in range(ROWS_Y):
        y_to = lax.rem(y + d, ROWS_Y)
        for s in range(2):
            src = act_in.at[:, pl.ds(pl.multiple_of((y_to + ROWS_Y * s) * HEAD, HEAD), HEAD)]
            dst = acts.at[x, core, y, :, pl.ds(s * HEAD, HEAD)]
            if d == 0:
                local(src, dst, ACT1).start()
            else:
                remote(src, dst, ACT1, (z * ROWS_Y + y_to) * 2 + core).start()

    wanted = columns[...]
    step_rows = 64
    for r in range(0, BLOCK, step_rows):
        row = lax.broadcasted_iota(jnp.int32, (step_rows, CHIPS * PICKS * PIECE), 0) + r
        col = lax.broadcasted_iota(jnp.int32, (step_rows, CHIPS * PICKS * PIECE), 1)
        hit = (row // PIECE == wanted) & (row % PIECE == col % PIECE)
        member[pl.ds(r, step_rows), :] = jnp.where(hit, 1.0, 0.0).astype(BF16)

    arrived(held, P1)

    def serve(d, carry):
        target = lax.rem(chip + d, CHIPS)
        for j in range(PICKS):
            picked[target, j] = held[table[target, j]]

        @pl.when(target != chip)
        def _():
            remote(picked.at[target], kv.at[core, chip], P2, target * 2 + core).start()

        @pl.when(target == chip)
        def _():
            local(picked.at[target], kv.at[core, chip], P2).start()

        return carry

    lax.fori_loop(0, CHIPS, serve, 0)

    arrived(acts.at[x, core], ACT1)
    for d in range(1, ROWS_X):
        x_to = lax.rem(x + d, ROWS_X)
        remote(acts.at[x, core], acts.at[x, core], ALONG_X + d, c, x_to).start()

    arrived(own, OWN)
    arrived(qd, LOAD)

    arrived(kv.at[core], P2)
    remote(kv.at[core], kv.at[core], SWAP, sibling).start()
    arrived(kv.at[other], SWAP)

    def lines(kind, j):
        if j == PICKS:
            return own[kind]
        return kv[kind, :, j].reshape(BLOCK, HEAD)

    for j in range(PICKS + 1):
        key_t[j] = lines(0, j).T

    alive = [live[chip, j] != 0 for j in range(PICKS)]

    def one_head(h, carry):
        block = pl.ds(pl.multiple_of(h * HALF, HALF), HALF)
        strip = pl.ds(pl.multiple_of(h * HEAD, HEAD), HEAD)
        queries = qd[0, block, :]
        grads_out = qd[1, block, :]
        peak = None
        for j in range(PICKS + 1):
            raw = rows_dot(lines(0, j), queries)
            if j == PICKS:
                key_at = lax.broadcasted_iota(jnp.int32, raw.shape, 0)
                query_at = lax.broadcasted_iota(jnp.int32, raw.shape, 1) + core * HALF
                raw = jnp.where(key_at <= query_at, raw, LOW)
            scores[j] = raw
            top = jnp.max(raw, axis=0, keepdims=True)
            if j < PICKS:
                top = jnp.where(alive[j], top, LOW)
            peak = top if peak is None else jnp.maximum(peak, top)
        total = jnp.zeros((1, HALF), F32)
        for j in range(PICKS + 1):
            base = peak if j == PICKS else jnp.where(alive[j], peak, HIGH)
            weights = jnp.exp2((scores[j] - base) * EXP_SCALE)
            scores[j] = weights
            total = total + jnp.sum(weights, axis=0, keepdims=True)
        share = 1.0 / total
        delta = jnp.zeros((1, HALF), F32)
        for j in range(PICKS + 1):
            gp = rows_dot(lines(1, j), grads_out)
            gprobs[j] = gp
            delta = delta + jnp.sum(scores[j] * gp, axis=0, keepdims=True)
        delta = delta * share
        dq = jnp.zeros((HEAD, HALF), F32)
        for j in range(PICKS + 1):
            probs = scores[j] * share
            low[1, j, :, block] = probs.astype(BF16)
            gs = (probs * (gprobs[j] - delta)).astype(BF16)
            low[0, j, :, block] = gs
            dq = dq + plain_dot(key_t[j], gs)
        dq_out[:, strip] = (dq * SCALE).T.astype(BF16)
        return carry

    lax.fori_loop(0, HEADS, one_head, 0)

    mine_scale = jnp.where(core == 0, SCALE, 1.0).astype(F32)
    other_scale = jnp.where(core == 0, 1.0, SCALE).astype(F32)
    for j in range(PICKS + 1):
        cross[j] = (plain_dot(low[other, j], qd[other]) * other_scale).astype(BF16)
        remote(cross.at[j], crossed.at[j], BACK0 + j, sibling).start()
    for j in range(PICKS):
        mine = plain_dot(low[core, j], qd[core]) * mine_scale
        arrived(crossed.at[j], BACK0 + j)
        mine = mine + crossed[j].astype(F32)
        terms[:, j] = mine.astype(BF16).reshape(CHIPS, PIECE, HEAD)

    def give(d, carry):
        target = lax.rem(chip + d, CHIPS)

        @pl.when(target != chip)
        def _():
            remote(terms.at[target], landed.at[chip], BACK2, target * 2 + core).start()

        @pl.when(target == chip)
        def _():
            local(terms.at[target], landed.at[chip], BACK2).start()

        return carry

    lax.fori_loop(0, CHIPS, give, 0)

    mine = plain_dot(low[core, PICKS], qd[core]) * mine_scale
    arrived(crossed.at[PICKS], BACK0 + PICKS)
    own_terms[...] = mine + crossed[PICKS].astype(F32)

    for d in range(1, ROWS_X):
        arrived(acts.at[lax.rem(x + ROWS_X - d, ROWS_X), core], ALONG_X + d)
    remote(acts.at[:, core], acts.at[:, core], ACT3, sibling).start()

    arrived(landed, BACK2)
    summed = plain_dot(member[...], landed[...].reshape(CHIPS * PICKS * PIECE, HEAD))
    sums[...] = summed.astype(BF16).reshape(CHIPS, PIECE, HEAD)

    def give_back(d, carry):
        target = lax.rem(chip + d, CHIPS)

        @pl.when(target != chip)
        def _():
            remote(sums.at[target], final.at[chip], BACK1, target * 2 + core).start()

        @pl.when(target == chip)
        def _():
            local(sums.at[target], final.at[chip], BACK1).start()

        return carry

    lax.fori_loop(0, CHIPS, give_back, 0)
    arrived(final, BACK1)
    grads[...] = (final[...].reshape(BLOCK, HEAD).astype(F32) + own_terms[...]).astype(BF16)

    for d in range(ROWS_Y):
        y_to = lax.rem(y + d, ROWS_Y)
        if d == 0:
            local(grads, all_grads.at[y], GATHER).start()
        else:
            remote(grads, all_grads.at[y], GATHER, (z * ROWS_Y + y_to) * 2 + core).start()
    their_rows = pl.ds(pl.multiple_of(other * HALF, HALF), HALF)
    remote(grads.at[their_rows], dkv_out.at[core], HALVES, sibling).start()
    local(grads.at[my_rows], dkv_out.at[core], HALVES).start()

    arrived(all_grads, GATHER)
    for half in range(2):
        for b in range(ROWS_Y):
            grads_t[:, pl.ds((half * ROWS_Y + b) * HALF, HALF)] = all_grads[
                b, pl.ds(half * HALF, HALF), :
            ].T
    arrived(acts.at[:, other], ACT3)
    for a in range(ROWS_X):
        both = plain_dot(grads_t[...], acts[a].reshape(2 * ROWS_Y * HALF, 2 * HEAD))
        wide[2 * a] = both[:, :HEAD]
        wide[2 * a + 1] = both[:, HEAD:]
        w_send[2 * a] = both[:, :HEAD].astype(BF16)
        w_send[2 * a + 1] = both[:, HEAD:].astype(BF16)
    for d in range(1, ROWS_Z):
        z_to = lax.rem(z + d, ROWS_Z)
        remote(w_send.at[z_to], wide_in.at[d - 1], SUMS, (z_to * ROWS_Y + y) * 2 + core).start()
    arrived(wide_in, SUMS)
    acc = wide[z]
    for d in range(ROWS_Z - 1):
        acc = acc + wide_in[d].astype(F32)
    w_rows[...] = acc.T
    keep = pl.ds(pl.multiple_of(core * (HEAD // 2), HEAD // 2), HEAD // 2)
    pass_on = pl.ds(pl.multiple_of(other * (HEAD // 2), HEAD // 2), HEAD // 2)
    remote(w_rows.at[pass_on], dw_out.at[core], LAST, sibling).start()
    local(w_rows.at[keep], dw_out.at[core], LAST).start()
    arrived(dw_out, LAST)
    arrived(dkv_out, HALVES)

    here = chip // (CHIPS // 2) == core

    @pl.when(here)
    def _():
        sent(held.at[pl.ds(0, CHIPS - 1)], P1)

    @pl.when(jnp.logical_not(here))
    def _():
        sent(held, P1)

    sent(own.at[:, pl.ds(0, HALF)], OWN)
    sent(acts.at[0, 0, pl.ds(0, ROWS_Y - 1)], ACT1)
    sent(kv.at[0, pl.ds(0, CHIPS - 1)], P2)
    sent(kv.at[0], SWAP)
    for d in range(1, ROWS_X):
        sent(acts.at[0, 0], ALONG_X + d)
    sent(acts.at[:, 0], ACT3)
    for j in range(PICKS + 1):
        sent(cross.at[j], BACK0 + j)
    sent(terms.at[pl.ds(0, CHIPS - 1)], BACK2)
    sent(sums.at[pl.ds(0, CHIPS - 1)], BACK1)
    sent(all_grads.at[pl.ds(0, ROWS_Y - 1)], GATHER)
    sent(dkv_out.at[0], HALVES)
    sent(w_send.at[pl.ds(0, ROWS_Z - 1)], SUMS)
    sent(dw_out.at[0], LAST)


def body(activations, queries, key_tensor, value_tensor, output_gradient, selection, block_order):
    blocks = jnp.arange(CHIPS, dtype=jnp.int32)
    holds = block_order[:, None] == blocks[None, :]
    asked = jnp.sum(jnp.where(holds[:, :, None], selection[None], 0), axis=1)
    live = (asked != block_order[:, None]).astype(jnp.int32)
    at = asked[:, :, None] == block_order[None, None, :]
    table = jnp.sum(jnp.where(at, blocks[None, None], 0), axis=2).astype(jnp.int32)
    columns = jnp.broadcast_to(table[:, :, None], (CHIPS, PICKS, PIECE)).reshape(1, -1)

    smem = pl.BlockSpec(memory_space=pltpu.SMEM)
    vmem = pl.BlockSpec(memory_space=pltpu.VMEM)
    anywhere = pl.BlockSpec(memory_space=pl.ANY)
    dq, dkv, dw = pl.pallas_call(
        kernel,
        out_shape=(
            jax.ShapeDtypeStruct((HALF, HEADS * HEAD), BF16),
            jax.ShapeDtypeStruct((2, HALF, HEAD), BF16),
            jax.ShapeDtypeStruct((2, HEAD // 2, HEAD), F32),
        ),
        in_specs=[smem, smem, vmem] + [anywhere] * 5,
        out_specs=[vmem] * 3,
        scratch_shapes=[
            pltpu.VMEM((2, QUERIES, HEAD), BF16),
            pltpu.VMEM((2, BLOCK, HEAD), BF16),
            pltpu.VMEM((CHIPS, PIECE, HEAD), BF16),
            pltpu.VMEM((CHIPS, PICKS, PIECE, HEAD), BF16),
            pltpu.VMEM((2, CHIPS, PICKS, PIECE, HEAD), BF16),
            pltpu.VMEM((PICKS + 1, HEAD, BLOCK), BF16),
            pltpu.VMEM((PICKS + 1, BLOCK, HALF), F32),
            pltpu.VMEM((PICKS + 1, BLOCK, HALF), F32),
            pltpu.VMEM((2, PICKS + 1, BLOCK, QUERIES), BF16),
            pltpu.VMEM((PICKS + 1, BLOCK, HEAD), BF16),
            pltpu.VMEM((PICKS + 1, BLOCK, HEAD), BF16),
            pltpu.VMEM((CHIPS, PICKS, PIECE, HEAD), BF16),
            pltpu.VMEM((CHIPS, PICKS, PIECE, HEAD), BF16),
            pltpu.VMEM((BLOCK, CHIPS * PICKS * PIECE), BF16),
            pltpu.VMEM((CHIPS, PIECE, HEAD), BF16),
            pltpu.VMEM((CHIPS, PIECE, HEAD), BF16),
            pltpu.VMEM((BLOCK, HEAD), F32),
            pltpu.VMEM((BLOCK, HEAD), BF16),
            pltpu.VMEM((ROWS_Y, BLOCK, HEAD), BF16),
            pltpu.VMEM((HEAD, ROWS_Y * BLOCK), BF16),
            pltpu.VMEM((ROWS_X, 2, ROWS_Y, HALF, 2 * HEAD), BF16),
            pltpu.VMEM((ROWS_Z, HEAD, HEAD), F32),
            pltpu.VMEM((ROWS_Z - 1, HEAD, HEAD), BF16),
            pltpu.VMEM((ROWS_Z, HEAD, HEAD), BF16),
            pltpu.VMEM((HEAD, HEAD), F32),
            pltpu.SemaphoreType.DMA((SEMS,)),
            pltpu.SemaphoreType.DMA((SEMS,)),
        ],
        compiler_params=pltpu.CompilerParams(
            collective_id=0, has_side_effects=True, vmem_limit_bytes=48 * 1024 * 1024
        ),
        name="attention_backward",
    )(
        table,
        live,
        columns,
        activations,
        queries,
        key_tensor,
        value_tensor,
        output_gradient,
    )
    return dq, dkv[0], dkv[1], dw[0], dw[1]


def solution(mesh):
    placed = (P("ctx", "tp"),) * 5 + (P(), P())
    return jax.shard_map(
        body,
        mesh=mesh,
        in_specs=placed,
        out_specs=(P("ctx", "tp"),) * 5,
        check_vma=False,
    )
```

time: 609 us -> 96.2 us (0.16)
  waiting for transfers between devices: 466 us -> 0 us
  Pallas kernels: 0 us -> 87.6 us
  local copies, waits for them, and re-layouts: 55.1 us -> 6.48 us
  other arithmetic: 28.5 us -> 1.17 us
  matrix products: 25 us -> 0 us
  between operations: 22.6 us -> 0.68 us
    reduce_scatter x1 -> x0, waiting for transfers between devices: 182 us -> none  [body(): lax.psum_scatter(accumulated[BLOCK_TOKENS:BLOCK_TOKENS + term_rows], 'ctx...]
    all_gather x3 -> x0, waiting for transfers between devices: 146 us -> none  [the longest x1 79.1 us: body(): lax.all_gather(value_tensor, 'ctx', axis=0, tiled=True)]
    unnamed x6 -> x0, waiting for transfers between devices: 138 us -> none
    pallas_call x0 -> x1, Pallas kernels: none -> 87.6 us  [body(): pl.pallas_call(kernel, out_shape=(jax.ShapeDtypeStruct((HALF, HEADS * HEA...]
    dot_general x25 -> x0, matrix products: 25 us -> none  [the longest x4 5.64 us: body(): jnp.einsum('gprl,rgpd->lgd', weights_low, grad_rows, preferred_element_ty...]
    concatenate x5 -> x0, other arithmetic: 15.7 us -> none  [the longest x1 13.6 us: collect(): padded_values = jnp.concatenate([edge, pieces[1], edge], axis=0)]
    slice x5 -> x0, local copies, waits for them, and re-layouts: 14.5 us -> none  [the longest x1 11.3 us: body(): accumulated[BLOCK_TOKENS:BLOCK_TOKENS + term_rows]]
    dynamic_update_slice x6 -> x0, local copies, waits for them, and re-layouts: 12 us -> none  [the longest x4 11.8 us: add_block(): lax.dynamic_update_slice_in_dim(total, old_rows + both_blocks[block_numbe...]
  transfers between devices with their start and end apart: 5 -> 0, of which waited for: 4 -> 0; matrix products, arithmetic and copies ran while one was open for 2% -> 0% of each run, Pallas kernels for 0% -> 0%
where the time goes in v1:
time: 96.2 us; the launch traced here: 95.9 us
  Pallas kernels  87.6 us (91%)
  local copies, waits for them, and re-layouts  6.48 us (7%)
  other arithmetic  1.17 us (1%)
    pallas_call x1, Pallas kernels, body(): pl.pallas_call(kernel, out_shape=(jax.ShapeDtypeStruct((HALF, HEADS * HEA...  87.6 us
    unnamed x15, local copies, waits for them, and re-layouts  4.81 us

profile of v1, /device:TPU:1, one launch (start us, length us, event | category | flops | bytes accessed | tf_op | source)
XLA Modules:
  0.0 95.9 jit_solution(7035778371429907743)
XLA Ops:
  0.6 0.0 copy-start.6
  0.6 0.7 iota_compare_fusion
  1.4 0.0 copy-done.6
  1.4 0.0 copy-start.5
  1.4 0.1 select_reduce_fusion.1
  1.5 0.5 copy-done.5
  2.0 0.2 select_reduce_fusion
  2.2 0.1 copy.20.table
  2.3 0.1 copy.17
  2.4 0.1 compare_convert_fusion.live
  2.5 0.0 copy-start.3
  2.5 0.0 copy-start.4
  2.5 0.1 broadcast_in_dim.51
  2.6 0.1 reshape.38.columns
  2.7 0.6 copy-done.3
  3.3 0.0 copy-done.4
  3.4 0.0 copy-start
  3.4 1.0 %copy-done = bf16[256,1024]{1,0:T(8,128)(2,1)S(1)} copy-done((bf16[256,1024]{1,0:T(8,128)(2,1)S(1)}, bf16[256,1024]{1,0:T(8,128)(2,1)}, u32[]{:S(2)}) %copy-start) | copy-done | bytes 524312
  4.4 0.0 copy-start.1
  4.4 0.9 copy-done.1
  5.4 0.0 copy-start.2
  5.4 0.9 copy-done.2
  6.3 87.6 %attention_backward.1 = (bf16[256,512]{1,0:T(8,128)(2,1)S(1)}, bf16[2,256,128]{2,1,0:T(8,128)(2,1)S(1)}, f32[2,64,128]{2,1,0:T(8,128)S(1)}) custom-call(s32[32,3]{1,0:T(8,128)S(1)} %copy.20.table, s32[32,3]{1,0:T(8,128)S(1)} %compare_convert_fusion.live, s32[1,1536]{1,0:T(1,128)S(1)} %reshape.38.columns, bf16[256,1024]{1,0:T(8,128)(2,1)S(1)} %copy-done, ...), custom_call_target="tpu_custom_call" | custom-call | tf_op jit(solution)/shard_map/attention_backward/pallas_call | solution.py:390
  93.9 0.6 slice_bitcast_fusion.2
  94.6 0.7 slice_bitcast_fusion
  95.2 0.7 copy.22
Async XLA Ops:
  0.6 0.7 copy-start.6
  1.4 0.7 copy-start.5
  2.5 0.8 copy-start.3
  2.5 0.9 copy-start.4
  3.4 1.0 %copy-start = (bf16[256,1024]{1,0:T(8,128)(2,1)S(1)}, bf16[256,1024]{1,0:T(8,128)(2,1)}, u32[]{:S(2)}) copy-start(bf16[256,1024]{1,0:T(8,128)(2,1)} %act_in.1) | copy-start | bytes 1572868
  4.4 0.9 copy-start.1
  5.4 0.9 copy-start.2

commit v2 on v1

v2 whole, which is shorter than its diff:
```python
import functools
import math

import jax
import jax.numpy as jnp
from jax import lax
from jax.experimental import pallas as pl
from jax.experimental.pallas import tpu as pltpu
from jax.sharding import PartitionSpec as P

MESH = pl.DeviceIdType.MESH
F32 = jnp.float32
BF16 = jnp.bfloat16

HEAD = 128
BLOCK = 512
HALF = 256
PICKS = 3
CHIPS = 32
ROWS_Y = 4
ROWS_Z = 8
ROWS_X = 4
CLASSES = 16
REPLICAS = 2
PIECE = BLOCK // CLASSES
CHUNKS = 4
CHUNK = BLOCK // CHUNKS
HEADS = 4
QUERIES = HEADS * HALF
SCALE = HEAD**-0.5
EXP_SCALE = SCALE * math.log2(math.e)
LOW = -1e30

(LOAD, P1, OWN, ACT1, ACT3, HALVES, SUMS, LISTS, ORDER, DQ) = range(10)
P2 = 10
SWAP = P2 + PICKS
BACK0 = SWAP + PICKS
ALONG_X = BACK0 + PICKS + 1
BACK2 = ALONG_X + ROWS_X
BACK1 = BACK2 + PICKS
GATHER = BACK1 + CHUNKS
SEMS = GATHER + CHUNKS


def rows_dot(left, right):
    return lax.dot_general(left, right, (((1,), (1,)), ((), ())), preferred_element_type=F32)


def plain_dot(left, right):
    return lax.dot_general(left, right, (((1,), (0,)), ((), ())), preferred_element_type=F32)


def kernel(
    act_in,
    q_in,
    k_in,
    v_in,
    go_in,
    selection_in,
    order_in,
    dq_out,
    dkv_out,
    dw_out,
    qd,
    own,
    held,
    picked,
    kv,
    key_t,
    exps,
    gprobs,
    stats,
    factors,
    delta,
    low,
    cross,
    crossed,
    terms,
    landed,
    member,
    totals,
    sums,
    final,
    own_terms,
    dq_t,
    dq_rows,
    grads,
    all_grads,
    grads_t,
    acts,
    wide,
    w_send,
    wide_in,
    selection,
    order,
    inverse,
    table,
    send,
    recv,
):
    c = lax.axis_index("ctx")
    x = lax.axis_index("tp")
    chip = c // 2
    core = c % 2
    z = chip // ROWS_Y
    y = chip % ROWS_Y
    other = 1 - core
    sibling = c + 1 - 2 * core
    piece_class = chip % CLASSES
    first_z = z + ROWS_Z - 1 - core

    def remote(src, dst, sem, ctx, tp=None):
        return pltpu.make_async_remote_copy(
            src_ref=src,
            dst_ref=dst,
            send_sem=send.at[sem],
            recv_sem=recv.at[sem],
            device_id=(ctx, x if tp is None else tp),
            device_id_type=MESH,
        )

    def local(src, dst, sem):
        return pltpu.make_async_copy(src, dst, recv.at[sem])

    def put(src, dst, sem, ctx):
        @pl.when(ctx != c)
        def _():
            remote(src, dst, sem, ctx).start()

        @pl.when(ctx == c)
        def _():
            local(src, dst, sem).start()

    coming = {}
    leaving = []

    def expect(sem, arrives, leaves=None):
        coming[sem] = arrives
        if leaves is not None:
            leaving.append((sem, leaves))

    def take(ref, sem):
        pltpu.make_async_copy(ref, ref, recv.at[sem]).wait()

    def arrived(sem):
        take(coming.pop(sem), sem)

    def sent(ref, sem):
        pltpu.make_async_copy(ref, ref, send.at[sem]).wait()

    def finish():
        for sem in list(coming):
            arrived(sem)
        for sem, ref in leaving:
            if ref is held:
                here = piece_class // (CLASSES // 2) == core

                @pl.when(here)
                def _():
                    sent(ref.at[pl.ds(0, CHIPS - 1)], sem)

                @pl.when(jnp.logical_not(here))
                def _():
                    sent(ref, sem)
            else:
                sent(ref, sem)

    barrier = pltpu.get_barrier_semaphore()

    def greet(d, carry):
        pl.semaphore_signal(
            barrier, inc=1, device_id=(lax.rem(c + d, 2 * CHIPS), x), device_id_type=MESH
        )
        return carry

    lax.fori_loop(1, 2 * CHIPS, greet, 0)
    for d in range(1, ROWS_X):
        pl.semaphore_signal(
            barrier, inc=1, device_id=(c, lax.rem(x + d, ROWS_X)), device_id_type=MESH
        )

    local(selection_in, selection, LISTS).start()
    local(order_in, order, ORDER).start()
    expect(LISTS, selection)
    expect(ORDER, order)
    for h in range(HEADS):
        strip = pl.ds(h * HEAD, HEAD)
        block = pl.ds(h * HALF, HALF)
        local(q_in.at[:, strip], qd.at[0, block], LOAD).start()
        local(go_in.at[:, strip], qd.at[1, block], LOAD).start()
    expect(LOAD, qd)

    pl.semaphore_wait(barrier, 2 * CHIPS - 1 + ROWS_X - 1)

    def spread(j, carry):
        rows = pl.ds(pl.multiple_of(j * PIECE, PIECE), PIECE)
        for replica in range(REPLICAS):
            holder = core * (CLASSES // 2) + j + CLASSES * replica
            for kind, src in ((0, k_in), (1, v_in)):
                put(src.at[rows], held.at[chip], P1, holder * 2 + kind)
        return carry

    lax.fori_loop(0, CLASSES // 2, spread, 0)
    expect(P1, held, held)

    my_rows = pl.ds(pl.multiple_of(core * HALF, HALF), HALF)
    for kind, src in ((0, k_in), (1, v_in)):
        remote(src, own.at[kind, my_rows], OWN, sibling).start()
        local(src, own.at[kind, my_rows], OWN).start()
    expect(OWN, own, own.at[:, pl.ds(0, HALF)])

    for d in range(ROWS_Y):
        y_to = lax.rem(y + d, ROWS_Y)
        for s in range(2):
            src = act_in.at[:, pl.ds(pl.multiple_of((y_to + ROWS_Y * s) * HEAD, HEAD), HEAD)]
            dst = acts.at[x, core, y, :, pl.ds(s * HEAD, HEAD)]
            if d == 0:
                local(src, dst, ACT1).start()
            else:
                remote(src, dst, ACT1, (z * ROWS_Y + y_to) * 2 + core).start()
    expect(ACT1, acts.at[x, core], acts.at[0, 0, pl.ds(0, ROWS_Y - 1)])

    arrived(ORDER)
    arrived(LISTS)

    def invert(e, carry):
        at = jnp.int32(0)
        for b in range(CHIPS):
            at = jnp.where(order[b] == e, b, at)
        inverse[e] = at
        return carry

    lax.fori_loop(0, CHIPS, invert, 0)

    def look_up(t, carry):
        for j in range(PICKS):
            table[t, j] = inverse[selection[j, order[t]]]
        return carry

    lax.fori_loop(0, CHIPS, look_up, 0)
    arrived(P1)

    for j in range(PICKS):

        def serve(n, carry, j=j):
            z_to = lax.rem(first_z + n // ROWS_Y, ROWS_Z)
            target = z_to * ROWS_Y + lax.rem(y + n, ROWS_Y)
            picked[j, n] = held[table[target, j]]
            put(picked.at[j, n], kv.at[core, j, piece_class], P2 + j, target * 2 + core)
            return carry

        lax.fori_loop(0, CLASSES, serve, 0)
        expect(P2 + j, kv.at[core, j], kv.at[0, 0, pl.ds(0, CLASSES - 1)])

    arrived(ACT1)
    for d in range(1, ROWS_X):
        x_to = lax.rem(x + d, ROWS_X)
        remote(acts.at[x, core], acts.at[x, core], ALONG_X + d, c, x_to).start()
        x_from = lax.rem(x + ROWS_X - d, ROWS_X)
        expect(ALONG_X + d, acts.at[x_from, core], acts.at[0, 0])

    def lines(kind, j):
        if j == PICKS:
            return own[kind]
        return kv[kind, j].reshape(BLOCK, HEAD)

    def forward(j):
        keys = lines(0, j)
        values = lines(1, j)
        key_t[j] = keys.T

        def one_head(h, carry):
            block = pl.ds(pl.multiple_of(h * HALF, HALF), HALF)
            raw = rows_dot(keys, qd[0, block, :])
            if j == PICKS:
                key_at = lax.broadcasted_iota(jnp.int32, raw.shape, 0)
                query_at = lax.broadcasted_iota(jnp.int32, raw.shape, 1) + core * HALF
                raw = jnp.where(key_at <= query_at, raw, LOW)
            top = jnp.max(raw, axis=0, keepdims=True)
            weights = jnp.exp2((raw - top) * EXP_SCALE)
            gp = rows_dot(values, qd[1, block, :])
            exps[j, :, block] = weights
            gprobs[j, :, block] = gp
            stats[j, 0, :, block] = top
            stats[j, 1, :, block] = jnp.sum(weights, axis=0, keepdims=True)
            stats[j, 2, :, block] = jnp.sum(weights * gp, axis=0, keepdims=True)
            return carry

        lax.fori_loop(0, HEADS, one_head, 0)

    arrived(OWN)
    arrived(LOAD)
    forward(PICKS)

    column = lax.broadcasted_iota(jnp.int32, (1, BLOCK), 1)
    step_rows = 2 * PIECE
    row = lax.broadcasted_iota(jnp.int32, (step_rows, BLOCK), 0)
    same = jnp.where(
        row % PIECE == lax.broadcasted_iota(jnp.int32, (step_rows, BLOCK), 1) % PIECE, 1.0, 0.0
    )
    for j in range(PICKS):
        wanted = jnp.zeros((1, BLOCK), jnp.int32)
        for n in range(CLASSES):
            client = lax.rem(first_z + n // ROWS_Y, ROWS_Z) * ROWS_Y + n % ROWS_Y
            wanted = jnp.where(column // PIECE == n, table[client, j], wanted)

        def fill(r, carry, j=j, wanted=wanted):
            hit = row // PIECE + 2 * r == wanted
            at = pl.ds(pl.multiple_of(r * step_rows, step_rows), step_rows)
            member[j, at, :] = jnp.where(hit, same, 0.0).astype(BF16)
            return carry

        lax.fori_loop(0, CHIPS // 2, fill, 0)

    def swap(j):
        arrived(P2 + j)
        remote(kv.at[core, j], kv.at[core, j], SWAP + j, sibling).start()
        expect(SWAP + j, kv.at[other, j], kv.at[0, 0])

    swap(0)
    swap(1)
    arrived(SWAP)
    forward(0)
    swap(2)
    arrived(SWAP + 1)
    forward(1)
    arrived(SWAP + 2)
    forward(2)

    mine_at = order[chip]
    alive = [selection[j, mine_at] != mine_at for j in range(PICKS)] + [True]
    peak = stats[PICKS, 0]
    for j in range(PICKS):
        peak = jnp.maximum(peak, jnp.where(alive[j], stats[j, 0], LOW))
    total = jnp.zeros((1, QUERIES), F32)
    turned = jnp.zeros((1, QUERIES), F32)
    scaled = []
    for j in range(PICKS + 1):
        part = jnp.exp2(jnp.minimum(stats[j, 0] - peak, 0.0) * EXP_SCALE)
        part = jnp.where(alive[j], part, 0.0)
        scaled.append(part)
        total = total + part * stats[j, 1]
        turned = turned + part * stats[j, 2]
    share = 1.0 / total
    delta[...] = turned * share
    for j in range(PICKS + 1):
        factors[j] = scaled[j] * share

    mine_scale = jnp.where(core == 0, SCALE, 1.0).astype(F32)
    other_scale = jnp.where(core == 0, 1.0, SCALE).astype(F32)

    def backward(j):
        keys_t = key_t[j]

        def one_head(h, carry):
            block = pl.ds(pl.multiple_of(h * HALF, HALF), HALF)
            probs = exps[j, :, block] * factors[j, :, block]
            gs = (probs * (gprobs[j, :, block] - delta[:, block])).astype(BF16)
            low[1, j, :, block] = probs.astype(BF16)
            low[0, j, :, block] = gs
            dq = plain_dot(keys_t, gs)
            dq_t[:, block] = dq if j == 0 else dq_t[:, block] + dq
            return carry

        lax.fori_loop(0, HEADS, one_head, 0)
        cross[j] = (plain_dot(low[other, j], qd[other]) * other_scale).astype(BF16)
        remote(cross.at[j], crossed.at[j], BACK0 + j, sibling).start()
        expect(BACK0 + j, crossed.at[j], cross.at[j])

    def combine(j):
        mine = plain_dot(low[core, j], qd[core]) * mine_scale
        arrived(BACK0 + j)
        return mine + crossed[j].astype(F32)

    def give(j):
        terms[j] = combine(j).astype(BF16).reshape(CLASSES, PIECE, HEAD)

        def one(n, carry):
            w = n // ROWS_Y
            z_to = lax.rem(z + ROWS_Z + 1 + core - w, ROWS_Z)
            holder = z_to * ROWS_Y + lax.rem(y + n, ROWS_Y)
            src = terms.at[j, lax.rem(holder, CLASSES)]
            put(src, landed.at[j, w * ROWS_Y + y], BACK2 + j, holder * 2 + core)
            return carry

        lax.fori_loop(0, CLASSES, one, 0)
        expect(BACK2 + j, landed.at[j], terms.at[0, pl.ds(0, CLASSES - 1)])

    backward(0)
    backward(1)
    give(0)
    backward(2)
    give(1)
    backward(PICKS)
    give(2)
    own_terms[...] = combine(PICKS)

    for h in range(HEADS):
        dq = dq_t[:, pl.ds(h * HALF, HALF)] * SCALE
        dq_rows[:, pl.ds(h * HEAD, HEAD)] = dq.T.astype(BF16)
    local(dq_rows, dq_out, DQ).start()
    expect(DQ, dq_out)

    for d in range(1, ROWS_X):
        arrived(ALONG_X + d)
    remote(acts.at[:, core], acts.at[:, core], ACT3, sibling).start()
    expect(ACT3, acts.at[:, other], acts.at[:, 0])

    for j in range(PICKS):
        arrived(BACK2 + j)
        part = plain_dot(member[j], landed[j].reshape(BLOCK, HEAD))
        if j == 0:
            totals[...] = part
        elif j < PICKS - 1:
            totals[...] += part
        else:
            sums[...] = (totals[...] + part).astype(BF16).reshape(CHIPS, PIECE, HEAD)

    def give_back(d, carry):
        target = lax.rem(chip + d, CHIPS)
        put(sums.at[target], final.at[chip], BACK1 + z % CHUNKS, target * 2 + core)
        return carry

    lax.fori_loop(0, CHIPS, give_back, 0)
    leaving.append((BACK1 + z % CHUNKS, sums.at[pl.ds(0, CHIPS - 1)]))

    def chunk_of(step):
        g = lax.rem(z + (2, 1, 3, 0)[step], CHUNKS)
        return g, pl.ds(pl.multiple_of(g * CHUNK, CHUNK), CHUNK)

    def collect(step):
        g, rows = chunk_of(step)
        take(final.at[pl.ds(0, 2 * ROWS_Y)], BACK1 + g)
        near = final[pl.ds(g * ROWS_Y, ROWS_Y)].astype(F32)
        far = final[pl.ds(CLASSES + g * ROWS_Y, ROWS_Y)].astype(F32)
        both = (near + far).reshape(CHUNK, HEAD) + own_terms[rows, :]
        grads[rows, :] = both.astype(BF16)
        for d in range(ROWS_Y):
            y_to = lax.rem(y + d, ROWS_Y)
            dst = all_grads.at[y, rows]
            if d == 0:
                local(grads.at[rows], dst, GATHER + step).start()
            else:
                to = (z * ROWS_Y + y_to) * 2 + core
                remote(grads.at[rows], dst, GATHER + step, to).start()
        expect(
            GATHER + step,
            all_grads.at[:, rows],
            all_grads.at[pl.ds(0, ROWS_Y - 1), pl.ds(0, CHUNK)],
        )

    def project(step):
        g, rows = chunk_of(step)
        arrived(GATHER + step)
        for b in range(ROWS_Y):
            grads_t[:, pl.ds(b * CHUNK, CHUNK)] = all_grads[b, rows, :].T
        half_rows = pl.ds(pl.multiple_of((g % 2) * CHUNK, CHUNK), CHUNK)
        for o in (2, 1, 3, 0):
            a = lax.rem(z // 2 + o, ROWS_X)
            part = plain_dot(
                grads_t[...], acts[a, g // 2, :, half_rows, :].reshape(ROWS_Y * CHUNK, 2 * HEAD)
            )
            if step == 0:
                wide[a] = part
                continue
            if step < CHUNKS - 1:
                wide[a] += part
                continue
            part = part + wide[a]
            for s in range(2):
                z_to = 2 * a + s
                w_send[z_to] = part[:, s * HEAD : (s + 1) * HEAD].T.astype(BF16)
                for h in range(2):
                    src = w_send.at[z_to, pl.ds(h * (HEAD // 2), HEAD // 2)]
                    to = (z_to * ROWS_Y + y) * 2 + h
                    put(src, wide_in.at[core, z], SUMS, to)

    collect(0)
    collect(1)
    arrived(ACT3)
    project(0)
    collect(2)
    project(1)
    collect(3)
    their_rows = pl.ds(pl.multiple_of(other * HALF, HALF), HALF)
    remote(grads.at[their_rows], dkv_out.at[core], HALVES, sibling).start()
    local(grads.at[my_rows], dkv_out.at[core], HALVES).start()
    expect(HALVES, dkv_out, dkv_out.at[0])
    project(2)
    project(3)
    expect(SUMS, wide_in, totals.at[pl.ds(0, (2 * ROWS_Z - 1) * HEAD // 4)])
    arrived(SUMS)
    for kind in range(2):
        acc = wide_in[kind, 0].astype(F32)
        for d in range(1, ROWS_Z):
            acc = acc + wide_in[kind, d].astype(F32)
        dw_out[kind] = acc
    finish()


def copy_kernel(dq, dkv, dw, dq_out, dk_out, dv_out, dwk_out, dwv_out, sems):
    copies = [
        pltpu.make_async_copy(src, dst, sems.at[n])
        for n, (src, dst) in enumerate(
            (
                (dq, dq_out),
                (dkv.at[0], dk_out),
                (dkv.at[1], dv_out),
                (dw.at[0], dwk_out),
                (dw.at[1], dwv_out),
            )
        )
    ]
    for one in copies:
        one.start()
    for one in copies:
        one.wait()


def body(activations, queries, key_tensor, value_tensor, output_gradient, selection, block_order):
    vmem = pl.BlockSpec(memory_space=pltpu.VMEM)
    hbm = pl.BlockSpec(memory_space=pltpu.HBM)
    dq, dkv, dw = pl.pallas_call(
        kernel,
        out_shape=(
            jax.ShapeDtypeStruct((HALF, HEADS * HEAD), BF16),
            jax.ShapeDtypeStruct((2, HALF, HEAD), BF16),
            jax.ShapeDtypeStruct((2, HEAD // 2, HEAD), F32),
        ),
        in_specs=[hbm] * 7,
        out_specs=[hbm, hbm, vmem],
        scratch_shapes=[
            pltpu.VMEM((2, QUERIES, HEAD), BF16),
            pltpu.VMEM((2, BLOCK, HEAD), BF16),
            pltpu.VMEM((CHIPS, PIECE, HEAD), BF16),
            pltpu.VMEM((PICKS, CLASSES, PIECE, HEAD), BF16),
            pltpu.VMEM((2, PICKS, CLASSES, PIECE, HEAD), BF16),
            pltpu.VMEM((PICKS + 1, HEAD, BLOCK), BF16),
            pltpu.VMEM((PICKS + 1, BLOCK, QUERIES), F32),
            pltpu.VMEM((PICKS + 1, BLOCK, QUERIES), F32),
            pltpu.VMEM((PICKS + 1, 3, 1, QUERIES), F32),
            pltpu.VMEM((PICKS + 1, 1, QUERIES), F32),
            pltpu.VMEM((1, QUERIES), F32),
            pltpu.VMEM((2, PICKS + 1, BLOCK, QUERIES), BF16),
            pltpu.VMEM((PICKS + 1, BLOCK, HEAD), BF16),
            pltpu.VMEM((PICKS + 1, BLOCK, HEAD), BF16),
            pltpu.VMEM((PICKS, CLASSES, PIECE, HEAD), BF16),
            pltpu.VMEM((PICKS, CLASSES, PIECE, HEAD), BF16),
            pltpu.VMEM((PICKS, CHIPS * PIECE, BLOCK), BF16),
            pltpu.VMEM((CHIPS * PIECE, HEAD), F32),
            pltpu.VMEM((CHIPS, PIECE, HEAD), BF16),
            pltpu.VMEM((CHIPS, PIECE, HEAD), BF16),
            pltpu.VMEM((BLOCK, HEAD), F32),
            pltpu.VMEM((HEAD, QUERIES), F32),
            pltpu.VMEM((HALF, HEADS * HEAD), BF16),
            pltpu.VMEM((BLOCK, HEAD), BF16),
            pltpu.VMEM((ROWS_Y, BLOCK, HEAD), BF16),
            pltpu.VMEM((HEAD, ROWS_Y * CHUNK), BF16),
            pltpu.VMEM((ROWS_X, 2, ROWS_Y, HALF, 2 * HEAD), BF16),
            pltpu.VMEM((ROWS_X, HEAD, 2 * HEAD), F32),
            pltpu.VMEM((ROWS_Z, HEAD, HEAD), BF16),
            pltpu.VMEM((2, ROWS_Z, HEAD // 2, HEAD), BF16),
            pltpu.SMEM((PICKS, CHIPS), jnp.int32),
            pltpu.SMEM((CHIPS,), jnp.int32),
            pltpu.SMEM((CHIPS,), jnp.int32),
            pltpu.SMEM((CHIPS, PICKS), jnp.int32),
            pltpu.SemaphoreType.DMA((SEMS,)),
            pltpu.SemaphoreType.DMA((SEMS,)),
        ],
        compiler_params=pltpu.CompilerParams(
            collective_id=0, has_side_effects=True, vmem_limit_bytes=56 * 1024 * 1024
        ),
        name="attention_backward",
    )(
        activations,
        queries,
        key_tensor,
        value_tensor,
        output_gradient,
        selection.T,
        block_order,
    )
    shapes = (dq.shape, dkv.shape[1:], dkv.shape[1:], dw.shape[1:], dw.shape[1:])
    kinds = (BF16, BF16, BF16, F32, F32)
    return pl.pallas_call(
        copy_kernel,
        out_shape=tuple(jax.ShapeDtypeStruct(s, t) for s, t in zip(shapes, kinds)),
        in_specs=[hbm] * 3,
        out_specs=[hbm] * 5,
        scratch_shapes=[pltpu.SemaphoreType.DMA((5,))],
        name="copy_out",
    )(dq, dkv, dw)


def solution(mesh):
    placed = (P("ctx", "tp"),) * 5 + (P(), P())
    return jax.shard_map(
        body,
        mesh=mesh,
        in_specs=placed,
        out_specs=(P("ctx", "tp"),) * 5,
        check_vma=False,
    )
```

time: 96.2 us -> 93.6 us (0.973)
  local copies, waits for them, and re-layouts: 6.48 us -> 0 us
  Pallas kernels: 87.6 us -> 92.9 us
  other arithmetic: 1.17 us -> 0 us
    pallas_call x0 -> x1, Pallas kernels: none -> 15 us  [body(): pl.pallas_call(copy_kernel, out_shape=tuple((jax.ShapeDtypeStruct(s, t) f...]
    pallas_call x1, Pallas kernels: 87.6 us -> 77.8 us  [body(): pl.pallas_call(kernel, out_shape=(jax.ShapeDtypeStruct((HALF, HEADS * HEA...]
    unnamed x15 -> x0, local copies, waits for them, and re-layouts: 4.81 us -> none
    squeeze x2 -> x0, local copies, waits for them, and re-layouts: 1.29 us -> none  [body(): return (dq, dkv[0], dkv[1], dw[0], dw[1])]
where the time goes in v2:
time: 93.6 us; the launch traced here: 93.5 us
  Pallas kernels  92.9 us (99%)
    pallas_call x1, Pallas kernels, body(): pl.pallas_call(kernel, out_shape=(jax.ShapeDtypeStruct((HALF, HEADS * HEA...  77.8 us
    pallas_call x1, Pallas kernels, body(): pl.pallas_call(copy_kernel, out_shape=tuple((jax.ShapeDtypeStruct(s, t) f...  15 us

profile of v2, /device:TPU:1, one launch (start us, length us, event | category | flops | bytes accessed | tf_op | source)
XLA Modules:
  0.0 93.5 jit_solution(14690677311414349185)
XLA Ops:
  0.6 77.8 %attention_backward.1 = (bf16[256,512]{1,0:T(8,128)(2,1)}, bf16[2,256,128]{2,1,0:T(8,128)(2,1)}, f32[2,64,128]{2,1,0:T(8,128)}) custom-call(bf16[256,1024]{1,0:T(8,128)(2,1)} %act_in.1, bf16[256,512]{1,0:T(8,128)(2,1)} %q_in.1, bf16[256,128]{1,0:T(8,128)(2,1)} %k_in.1, bf16[256,128]{1,0:T(8,128)(2,1)} %v_in.1, bf16[256,512]{1,0:T(8,128)(2,1)} %go_in.1, ...), custom_call_target="tpu_custom_call" | custom-call | tf_op jit(solution)/shard_map/attention_backward/pallas_call | solution.py:523
  78.5 15.0 %copy_out.1 = (bf16[256,512]{1,0:T(8,128)(2,1)}, bf16[256,128]{1,0:T(8,128)(2,1)}, bf16[256,128]{1,0:T(8,128)(2,1)}, f32[64,128]{1,0:T(8,128)}, f32[64,128]{1,0:T(8,128)}) custom-call(bf16[256,512]{1,0:T(8,128)(2,1)} %get-tuple-element.8.dq, bf16[2,256,128]{2,1,0:T(8,128)(2,1)} %get-tuple-element.9.dkv, f32[2,64,128]{2,1,0:T(8,128)} %get-tuple-element.10.dw), custom_call_target="tpu_custom_call" | custom-call | tf_op jit(solution)/shard_map/copy_out/pallas_call | solution.py:585

commit v3 on v2

v3 whole, which is shorter than its diff:
```python
import functools
import math

import jax
import jax.numpy as jnp
from jax import lax
from jax.experimental import pallas as pl
from jax.experimental.pallas import tpu as pltpu
from jax.sharding import PartitionSpec as P

MESH = pl.DeviceIdType.MESH
F32 = jnp.float32
BF16 = jnp.bfloat16

HEAD = 128
BLOCK = 512
HALF = 256
PICKS = 3
CHIPS = 32
ROWS_Y = 4
ROWS_Z = 8
ROWS_X = 4
CLASSES = 16
REPLICAS = 2
PIECE = HALF // CLASSES
CHUNKS = 4
CHUNK = HALF // CHUNKS
TERMS = CLASSES * PIECE
HEADS = 4
QUERIES = HEADS * BLOCK
SCALE = HEAD**-0.5
EXP_SCALE = SCALE * math.log2(math.e)
LOW = -1e30

(LOAD, P1, PACK, ACT1, ACT3, STATS, SUMS, LISTS, ORDER, DQ, DQ_PART, DKV) = range(12)
P2 = 12
ALONG_X = P2 + PICKS
BACK2 = ALONG_X + ROWS_X
BACK1 = BACK2 + PICKS
GATHER = BACK1 + CHUNKS
SEMS = GATHER + CHUNKS


def rows_dot(left, right):
    return lax.dot_general(left, right, (((1,), (1,)), ((), ())), preferred_element_type=F32)


def plain_dot(left, right):
    return lax.dot_general(left, right, (((1,), (0,)), ((), ())), preferred_element_type=F32)


def kernel(
    act_in,
    q_in,
    k_in,
    v_in,
    go_in,
    selection_in,
    order_in,
    dq_out,
    dkv_out,
    dw_out,
    qd,
    packed,
    held,
    picked,
    kv,
    key_t,
    exps,
    gprobs,
    stats,
    my_stats,
    their_stats,
    factors,
    delta,
    low,
    terms,
    landed,
    member,
    totals,
    sums,
    final,
    own_terms,
    dq_mine,
    dq_give,
    dq_got,
    dq_rows,
    grads,
    all_grads,
    grads_t,
    acts,
    wide,
    w_send,
    wide_in,
    selection,
    order,
    inverse,
    table,
    send,
    recv,
):
    c = lax.axis_index("ctx")
    x = lax.axis_index("tp")
    chip = c // 2
    core = c % 2
    z = chip // ROWS_Y
    y = chip % ROWS_Y
    other = 1 - core
    sibling = c + 1 - 2 * core
    piece_class = chip % CLASSES
    served = (2 + 4 * core, ROWS_Z - 1, 1, 0)

    def chip_at(dz, dy):
        return lax.rem(z + dz, ROWS_Z) * ROWS_Y + lax.rem(y + dy, ROWS_Y)

    def remote(src, dst, sem, ctx, tp=None):
        return pltpu.make_async_remote_copy(
            src_ref=src,
            dst_ref=dst,
            send_sem=send.at[sem],
            recv_sem=recv.at[sem],
            device_id=(ctx, x if tp is None else tp),
            device_id_type=MESH,
        )

    def local(src, dst, sem):
        return pltpu.make_async_copy(src, dst, recv.at[sem])

    def put(src, dst, sem, ctx, here):
        if here:
            local(src, dst, sem).start()
        else:
            remote(src, dst, sem, ctx).start()

    coming = {}
    leaving = []

    def expect(sem, arrives, leaves=None):
        coming[sem] = arrives
        if leaves is not None:
            leaving.append((sem, leaves))

    def take(ref, sem):
        pltpu.make_async_copy(ref, ref, recv.at[sem]).wait()

    def arrived(sem):
        take(coming.pop(sem), sem)

    def sent(ref, sem):
        pltpu.make_async_copy(ref, ref, send.at[sem]).wait()

    def finish():
        for sem in list(coming):
            arrived(sem)
        for sem, ref in leaving:
            sent(ref, sem)

    barrier = pltpu.get_barrier_semaphore()

    def greet(d, carry):
        pl.semaphore_signal(
            barrier, inc=1, device_id=(lax.rem(c + d, 2 * CHIPS), x), device_id_type=MESH
        )
        return carry

    lax.fori_loop(1, 2 * CHIPS, greet, 0)
    for d in range(1, ROWS_X):
        pl.semaphore_signal(
            barrier, inc=1, device_id=(c, lax.rem(x + d, ROWS_X)), device_id_type=MESH
        )

    local(selection_in, selection, LISTS).start()
    local(order_in, order, ORDER).start()
    expect(LISTS, selection)
    expect(ORDER, order)
    for kind, src in ((0, k_in), (1, v_in)):
        local(src, packed.at[:, kind], PACK).start()
    expect(PACK, packed)
    arrived(PACK)

    pl.semaphore_wait(barrier, 2 * CHIPS - 1 + ROWS_X - 1)

    far_first = (4, 3, 5, 2, 6, 1, 7, 0)
    for dz in far_first:
        for dy in (2, 1, 3, 0):
            target = chip_at(dz, dy)
            src = packed.at[lax.rem(target, CLASSES)]
            put(src, held.at[chip], P1, target * 2 + core, dz == 0 and dy == 0)
    expect(P1, held, held.at[pl.ds(0, CHIPS - 1)])

    for h in range(HEADS):
        strip = pl.ds(h * HEAD, HEAD)
        rows = pl.ds(pl.multiple_of(h * BLOCK + core * HALF, HALF), HALF)
        for kind, src in ((0, q_in), (1, go_in)):
            remote(src.at[:, strip], qd.at[kind, rows], LOAD, sibling).start()
            local(src.at[:, strip], qd.at[kind, rows], LOAD).start()
    expect(LOAD, qd, qd.at[0])

    arrived(ORDER)
    arrived(LISTS)

    def invert(e, carry):
        at = jnp.int32(0)
        for b in range(CHIPS):
            at = jnp.where(order[b] == e, b, at)
        inverse[e] = at
        return carry

    lax.fori_loop(0, CHIPS, invert, 0)

    def look_up(t, carry):
        for j in range(PICKS):
            table[t, j] = inverse[selection[j, order[t]]]
        return carry

    lax.fori_loop(0, CHIPS, look_up, 0)
    def lines(kind, j):
        source = packed if j == PICKS else kv.at[j]
        return source[:, kind].reshape(HALF, HEAD)

    def forward(j):
        keys = lines(0, j)
        values = lines(1, j)
        key_t[:, pl.ds(j * HALF, HALF)] = keys.T
        for h in range(HEADS):
            block = pl.ds(h * BLOCK, BLOCK)
            raw = rows_dot(keys, qd[0, block, :])
            if j == PICKS:
                key_at = lax.broadcasted_iota(jnp.int32, raw.shape, 0) + core * HALF
                query_at = lax.broadcasted_iota(jnp.int32, raw.shape, 1)
                raw = jnp.where(key_at <= query_at, raw, LOW)
            top = jnp.max(raw, axis=0, keepdims=True)
            weights = jnp.exp2((raw - top) * EXP_SCALE)
            gp = rows_dot(values, qd[1, block, :])
            exps[j, :, block] = weights
            gprobs[j, :, block] = gp
            stats[j, 0, :, block] = top
            stats[j, 1, :, block] = jnp.sum(weights, axis=0, keepdims=True)
            stats[j, 2, :, block] = jnp.sum(weights * gp, axis=0, keepdims=True)

    arrived(LOAD)
    forward(PICKS)

    for d in range(ROWS_Y):
        y_to = lax.rem(y + d, ROWS_Y)
        for s in range(2):
            src = act_in.at[:, pl.ds(pl.multiple_of((y_to + ROWS_Y * s) * HEAD, HEAD), HEAD)]
            dst = acts.at[x, core, y, :, pl.ds(s * HEAD, HEAD)]
            put(src, dst, ACT1, (z * ROWS_Y + y_to) * 2 + core, d == 0)
    expect(ACT1, acts.at[x, core], acts.at[0, 0, pl.ds(0, ROWS_Y - 1)])

    column = lax.broadcasted_iota(jnp.int32, (1, TERMS), 1)
    step_rows = 4 * PIECE
    row = lax.broadcasted_iota(jnp.int32, (step_rows, TERMS), 0)
    same = jnp.where(
        row % PIECE == lax.broadcasted_iota(jnp.int32, (step_rows, TERMS), 1) % PIECE, 1.0, 0.0
    )
    for j in range(PICKS):
        wanted = jnp.zeros((1, TERMS), jnp.int32)
        for n in range(CLASSES):
            client = chip_at(served[n // ROWS_Y], n % ROWS_Y)
            wanted = jnp.where(column // PIECE == n, table[client, j], wanted)

        def fill(r, carry, j=j, wanted=wanted):
            hit = row // PIECE + 4 * r == wanted
            at = pl.ds(pl.multiple_of(r * step_rows, step_rows), step_rows)
            member[j, at, :] = jnp.where(hit, same, 0.0).astype(BF16)
            return carry

        lax.fori_loop(0, CHIPS // 4, fill, 0)

    arrived(P1)

    for j in range(PICKS):
        for n in range(CLASSES):
            dz, dy = served[n // ROWS_Y], n % ROWS_Y
            target = chip_at(dz, dy)
            picked[j, n] = held[table[target, j]]
            dst = kv.at[j, piece_class]
            put(picked.at[j, n], dst, P2 + j, target * 2 + core, n == 3 * ROWS_Y)
        expect(P2 + j, kv.at[j], kv.at[0, pl.ds(0, CLASSES - 1)])

    arrived(ACT1)
    for d in range(1, ROWS_X):
        x_to = lax.rem(x + d, ROWS_X)
        remote(acts.at[x, core], acts.at[x, core], ALONG_X + d, c, x_to).start()
        x_from = lax.rem(x + ROWS_X - d, ROWS_X)
        expect(ALONG_X + d, acts.at[x_from, core], acts.at[0, 0])

    for j in range(PICKS):
        arrived(P2 + j)
        forward(j)

    mine_at = order[chip]
    alive = [selection[j, mine_at] != mine_at for j in range(PICKS)] + [True]

    def part_of(top, peak):
        return jnp.exp2(jnp.minimum(top - peak, 0.0) * EXP_SCALE)

    peak = stats[PICKS, 0]
    for j in range(PICKS):
        peak = jnp.maximum(peak, jnp.where(alive[j], stats[j, 0], LOW))
    total = jnp.zeros((1, QUERIES), F32)
    turned = jnp.zeros((1, QUERIES), F32)
    parts = []
    for j in range(PICKS + 1):
        part = jnp.where(alive[j], part_of(stats[j, 0], peak), 0.0)
        parts.append(part)
        total = total + part * stats[j, 1]
        turned = turned + part * stats[j, 2]
    my_stats[pl.ds(0, 1), :] = peak
    my_stats[pl.ds(1, 1), :] = total
    my_stats[pl.ds(2, 1), :] = turned
    remote(my_stats, their_stats, STATS, sibling).start()
    expect(STATS, their_stats, my_stats)
    arrived(STATS)
    their_peak = their_stats[pl.ds(0, 1), :]
    top = jnp.maximum(peak, their_peak)
    mine_part = part_of(peak, top)
    their_part = part_of(their_peak, top)
    share = 1.0 / (mine_part * total + their_part * their_stats[pl.ds(1, 1), :])
    delta[...] = (mine_part * turned + their_part * their_stats[pl.ds(2, 1), :]) * share
    for j in range(PICKS + 1):
        factors[j] = parts[j] * (mine_part * share)

    def backward(j):
        for h in range(HEADS):
            block = pl.ds(h * BLOCK, BLOCK)
            probs = exps[j, :, block] * factors[j, :, block]
            gs = probs * (gprobs[j, :, block] - delta[:, block])
            low[1, j, :, block] = probs.astype(BF16)
            low[0, j, :, block] = gs.astype(BF16)
        return plain_dot(low[0, j], qd[0]) * SCALE, plain_dot(low[1, j], qd[1])

    for j in range(PICKS):
        for kind, part in enumerate(backward(j)):
            terms[j, :, kind] = part.astype(BF16).reshape(CLASSES, PIECE, HEAD)
        for n in range(CLASSES):
            dz, dy = ROWS_Z - served[n // ROWS_Y], ROWS_Y - n % ROWS_Y
            holder = chip_at(dz, dy)
            src = terms.at[j, lax.rem(holder, CLASSES)]
            put(src, landed.at[j, n], BACK2 + j, holder * 2 + core, n == 3 * ROWS_Y)
        expect(BACK2 + j, landed.at[j], terms.at[0, pl.ds(0, CLASSES - 1)])
    for kind, part in enumerate(backward(PICKS)):
        own_terms[kind] = part

    for h in range(HEADS):
        gs = low[0, :, :, pl.ds(h * BLOCK, BLOCK)].reshape((PICKS + 1) * HALF, BLOCK)
        dq = plain_dot(key_t[...], gs)
        at = pl.ds(h * HALF, HALF)
        first, second = dq[:, :HALF], dq[:, HALF:]
        dq_mine[:, at] = jnp.where(core == 0, first, second)
        dq_give[:, at] = jnp.where(core == 0, second, first)
    remote(dq_give, dq_got, DQ_PART, sibling).start()
    expect(DQ_PART, dq_got, dq_give)

    for d in range(1, ROWS_X):
        arrived(ALONG_X + d)
    remote(acts.at[:, core], acts.at[:, core], ACT3, sibling).start()
    expect(ACT3, acts.at[:, other], acts.at[:, 0])

    for j in range(PICKS):
        arrived(BACK2 + j)
        both = [landed[j, :, kind].reshape(TERMS, HEAD) for kind in range(2)]
        part = plain_dot(member[j], jnp.concatenate(both, axis=1))
        if j == 0:
            totals[...] = part
        elif j < PICKS - 1:
            totals[...] += part
        else:
            part = (totals[...] + part).astype(BF16)
            for kind in range(2):
                strip = part[:, kind * HEAD : (kind + 1) * HEAD]
                sums[:, kind] = strip.reshape(CHIPS, PIECE, HEAD)

    group = z % CHUNKS
    for dz in (4, 0, 3, 7, 1, 5, 2, 6):
        for dy in (2, 1, 3, 0):
            target = chip_at(dz, dy)
            here = dz == 0 and dy == 0
            put(sums.at[target], final.at[chip], BACK1 + group, target * 2 + core, here)
    leaving.append((BACK1 + group, sums.at[pl.ds(0, CHIPS - 1)]))

    arrived(DQ_PART)
    for h in range(HEADS):
        at = pl.ds(h * HALF, HALF)
        dq = (dq_mine[:, at] + dq_got[:, at]) * SCALE
        dq_rows[:, pl.ds(h * HEAD, HEAD)] = dq.T.astype(BF16)
    local(dq_rows, dq_out, DQ).start()
    expect(DQ, dq_out)
    arrived(ACT3)

    def chunk_of(step):
        g = lax.rem(z + (0, 1, 3, 2)[step], CHUNKS)
        return g, pl.ds(pl.multiple_of(g * CHUNK, CHUNK), CHUNK)

    def collect(step):
        g, rows = chunk_of(step)
        take(final.at[pl.ds(0, 2 * ROWS_Y)], BACK1 + g)
        near = final[pl.ds(g * ROWS_Y, ROWS_Y)].astype(F32)
        far = final[pl.ds(CLASSES + g * ROWS_Y, ROWS_Y)].astype(F32)
        both = near + far
        for kind in range(2):
            whole = both[:, kind].reshape(CHUNK, HEAD) + own_terms[kind, rows, :]
            grads[kind, rows, :] = whole.astype(BF16)
        dst = all_grads.at[core, y, rows]
        for d in (2, 1, 3, 0):
            to = chip_at(0, d) * 2
            for swap in range(2):
                kind = core if swap == 0 else other
                put(grads.at[kind, rows], dst, GATHER + step, to + kind, d == 0 and swap == 0)
        expect(GATHER + step, all_grads.at[:, :, rows], held.at[pl.ds(0, 7 * CHUNK // (2 * PIECE))])

    def project(step):
        g, rows = chunk_of(step)
        arrived(GATHER + step)
        grads_t[...] = all_grads[:, :, rows, :].reshape(2 * ROWS_Y * CHUNK, HEAD).T
        for o in (2, 1, 3, 0):
            a = lax.rem(z // 2 + o, ROWS_X)
            features = acts[a, :, :, rows, :].reshape(2 * ROWS_Y * CHUNK, 2 * HEAD)
            part = plain_dot(grads_t[...], features)
            if step == 0:
                wide[a] = part
                continue
            if step < CHUNKS - 1:
                wide[a] += part
                continue
            part = part + wide[a]
            for s in range(2):
                z_to = 2 * a + s
                w_send[z_to] = part[:, s * HEAD : (s + 1) * HEAD].T.astype(BF16)
                for h in range(2):
                    src = w_send.at[z_to, pl.ds(h * (HEAD // 2), HEAD // 2)]
                    to = (z_to * ROWS_Y + y) * 2 + h
                    dst = wide_in.at[core, z]

                    @pl.when(to != c)
                    def _(src=src, dst=dst, to=to):
                        remote(src, dst, SUMS, to).start()

                    @pl.when(to == c)
                    def _(src=src, dst=dst):
                        local(src, dst, SUMS).start()

    for step in range(CHUNKS):
        collect(step)
    local(grads, dkv_out, DKV).start()
    expect(DKV, dkv_out)
    for step in range(CHUNKS - 1):
        project(step)
    project(3)
    expect(SUMS, wide_in, held.at[pl.ds(0, (2 * ROWS_Z - 1) * HEAD // (4 * PIECE))])
    arrived(SUMS)
    for kind in range(2):
        acc = wide_in[kind, 0].astype(F32)
        for d in range(1, ROWS_Z):
            acc = acc + wide_in[kind, d].astype(F32)
        dw_out[kind] = acc
    finish()


def copy_kernel(dq, dkv, dw, dq_out, dk_out, dv_out, dwk_out, dwv_out, sems):
    pairs = (
        (dq, dq_out),
        (dkv.at[0], dk_out),
        (dkv.at[1], dv_out),
        (dw.at[0], dwk_out),
        (dw.at[1], dwv_out),
    )
    copies = [pltpu.make_async_copy(src, dst, sems.at[n]) for n, (src, dst) in enumerate(pairs)]
    for one in copies:
        one.start()
    for one in copies:
        one.wait()


def body(activations, queries, key_tensor, value_tensor, output_gradient, selection, block_order):
    vmem = pl.BlockSpec(memory_space=pltpu.VMEM)
    hbm = pl.BlockSpec(memory_space=pltpu.HBM)
    dq, dkv, dw = pl.pallas_call(
        kernel,
        out_shape=(
            jax.ShapeDtypeStruct((HALF, HEADS * HEAD), BF16),
            jax.ShapeDtypeStruct((2, HALF, HEAD), BF16),
            jax.ShapeDtypeStruct((2, HEAD // 2, HEAD), F32),
        ),
        in_specs=[hbm] * 7,
        out_specs=[hbm, hbm, vmem],
        scratch_shapes=[
            pltpu.VMEM((2, QUERIES, HEAD), BF16),
            pltpu.VMEM((CLASSES, 2, PIECE, HEAD), BF16),
            pltpu.VMEM((CHIPS, 2, PIECE, HEAD), BF16),
            pltpu.VMEM((PICKS, CLASSES, 2, PIECE, HEAD), BF16),
            pltpu.VMEM((PICKS, CLASSES, 2, PIECE, HEAD), BF16),
            pltpu.VMEM((HEAD, (PICKS + 1) * HALF), BF16),
            pltpu.VMEM((PICKS + 1, HALF, QUERIES), F32),
            pltpu.VMEM((PICKS + 1, HALF, QUERIES), F32),
            pltpu.VMEM((PICKS + 1, 3, 1, QUERIES), F32),
            pltpu.VMEM((8, QUERIES), F32),
            pltpu.VMEM((8, QUERIES), F32),
            pltpu.VMEM((PICKS + 1, 1, QUERIES), F32),
            pltpu.VMEM((1, QUERIES), F32),
            pltpu.VMEM((2, PICKS + 1, HALF, QUERIES), BF16),
            pltpu.VMEM((PICKS, CLASSES, 2, PIECE, HEAD), BF16),
            pltpu.VMEM((PICKS, CLASSES, 2, PIECE, HEAD), BF16),
            pltpu.VMEM((PICKS, CHIPS * PIECE, TERMS), BF16),
            pltpu.VMEM((CHIPS * PIECE, 2 * HEAD), F32),
            pltpu.VMEM((CHIPS, 2, PIECE, HEAD), BF16),
            pltpu.VMEM((CHIPS, 2, PIECE, HEAD), BF16),
            pltpu.VMEM((2, HALF, HEAD), F32),
            pltpu.VMEM((HEAD, HEADS * HALF), F32),
            pltpu.VMEM((HEAD, HEADS * HALF), F32),
            pltpu.VMEM((HEAD, HEADS * HALF), F32),
            pltpu.VMEM((HALF, HEADS * HEAD), BF16),
            pltpu.VMEM((2, HALF, HEAD), BF16),
            pltpu.VMEM((2, ROWS_Y, HALF, HEAD), BF16),
            pltpu.VMEM((HEAD, 2 * ROWS_Y * CHUNK), BF16),
            pltpu.VMEM((ROWS_X, 2, ROWS_Y, HALF, 2 * HEAD), BF16),
            pltpu.VMEM((ROWS_X, HEAD, 2 * HEAD), F32),
            pltpu.VMEM((ROWS_Z, HEAD, HEAD), BF16),
            pltpu.VMEM((2, ROWS_Z, HEAD // 2, HEAD), BF16),
            pltpu.SMEM((PICKS, CHIPS), jnp.int32),
            pltpu.SMEM((CHIPS,), jnp.int32),
            pltpu.SMEM((CHIPS,), jnp.int32),
            pltpu.SMEM((CHIPS, PICKS), jnp.int32),
            pltpu.SemaphoreType.DMA((SEMS,)),
            pltpu.SemaphoreType.DMA((SEMS,)),
        ],
        compiler_params=pltpu.CompilerParams(
            collective_id=0, has_side_effects=True, vmem_limit_bytes=56 * 1024 * 1024
        ),
        name="attention_backward",
    )(
        activations,
        queries,
        key_tensor.reshape(CLASSES, PIECE, HEAD),
        value_tensor.reshape(CLASSES, PIECE, HEAD),
        output_gradient,
        selection.T,
        block_order,
    )
    shapes = (dq.shape, dkv.shape[1:], dkv.shape[1:], dw.shape[1:], dw.shape[1:])
    kinds = (BF16, BF16, BF16, F32, F32)
    return pl.pallas_call(
        copy_kernel,
        out_shape=tuple(jax.ShapeDtypeStruct(s, t) for s, t in zip(shapes, kinds)),
        in_specs=[hbm] * 3,
        out_specs=[vmem] * 5,
        scratch_shapes=[pltpu.SemaphoreType.DMA((5,))],
        name="copy_out",
    )(dq, dkv, dw)


def solution(mesh):
    placed = (P("ctx", "tp"),) * 5 + (P(), P())
    return jax.shard_map(
        body,
        mesh=mesh,
        in_specs=placed,
        out_specs=(P("ctx", "tp"),) * 5,
        check_vma=False,
    )
```

time: 93.6 us -> 79.3 us (0.85)
  Pallas kernels: 92.9 us -> 78.5 us
    pallas_call x1, Pallas kernels: 15 us -> 1.76 us  [body(): pl.pallas_call(copy_kernel, out_shape=tuple((jax.ShapeDtypeStruct(s, t) f...]
    pallas_call x1, Pallas kernels: 77.8 us -> 76.7 us  [body(): pl.pallas_call(kernel, out_shape=(jax.ShapeDtypeStruct((HALF, HEADS * HEA...]
where the time goes in v3:
time: 79.3 us; the launch traced here: 79.1 us
  Pallas kernels  78.5 us (99%)
    pallas_call x1, Pallas kernels, body(): pl.pallas_call(kernel, out_shape=(jax.ShapeDtypeStruct((HALF, HEADS * HEA...  76.7 us
    pallas_call x1, Pallas kernels, body(): pl.pallas_call(copy_kernel, out_shape=tuple((jax.ShapeDtypeStruct(s, t) f...  1.76 us

profile of v3, /device:TPU:1, one launch (start us, length us, event | category | flops | bytes accessed | tf_op | source)
XLA Modules:
  0.0 79.1 jit_solution(835762506784137583)
XLA Ops:
  0.6 76.7 %attention_backward.1 = (bf16[256,512]{1,0:T(8,128)(2,1)}, bf16[2,256,128]{2,1,0:T(8,128)(2,1)}, f32[2,64,128]{2,1,0:T(8,128)}) custom-call(bf16[256,1024]{1,0:T(8,128)(2,1)} %act_in.1, bf16[256,512]{1,0:T(8,128)(2,1)} %q_in.1, bf16[16,16,128]{2,1,0:T(8,128)(2,1)} %bitcast.3, bf16[16,16,128]{2,1,0:T(8,128)(2,1)} %bitcast.4, bf16[256,512]{1,0:T(8,128)(2,1)} %go_in.1, ...), custom_call_target="tpu_custom_call" | custom-call | tf_op jit(solution)/shard_map/attention_backward/pallas_call | solution.py:480
  77.4 1.8 %copy_out.1 = (bf16[256,512]{1,0:T(8,128)(2,1)}, bf16[256,128]{1,0:T(8,128)(2,1)}, bf16[256,128]{1,0:T(8,128)(2,1)}, f32[64,128]{1,0:T(8,128)}, f32[64,128]{1,0:T(8,128)}) custom-call(bf16[256,512]{1,0:T(8,128)(2,1)} %get-tuple-element.8.dq, bf16[2,256,128]{2,1,0:T(8,128)(2,1)} %get-tuple-element.9.dkv, f32[2,64,128]{2,1,0:T(8,128)} %get-tuple-element.10.dw), custom_call_target="tpu_custom_call" | custom-call | tf_op jit(solution)/shard_map/copy_out/pallas_call | solution.py:544

commit v4 on v3

--- a/solution.py
+++ b/solution.py
@@ -149,11 +149,20 @@
     def sent(ref, sem):
         pltpu.make_async_copy(ref, ref, send.at[sem]).wait()
 
+    todo = []
+
     def finish():
+        for st in todo:
+            g, rows = chunk_of(st)
+            take(final.at[pl.ds(0, 2 * ROWS_Y)], BACK1 + g)
         for sem in list(coming):
             arrived(sem)
         for sem, ref in leaving:
             sent(ref, sem)
+
+    def chunk_of(step):
+        g = lax.rem(z + (0, 1, 3, 2)[step], CHUNKS)
+        return g, pl.ds(pl.multiple_of(g * CHUNK, CHUNK), CHUNK)
 
     barrier = pltpu.get_barrier_semaphore()
 
@@ -187,6 +196,14 @@
             src = packed.at[lax.rem(target, CLASSES)]
             put(src, held.at[chip], P1, target * 2 + core, dz == 0 and dy == 0)
     expect(P1, held, held.at[pl.ds(0, CHIPS - 1)])
+
+    for d in range(ROWS_Y):
+        y_to = lax.rem(y + d, ROWS_Y)
+        for s in range(2):
+            src = act_in.at[:, pl.ds(pl.multiple_of((y_to + ROWS_Y * s) * HEAD, HEAD), HEAD)]
+            dst = acts.at[x, core, y, :, pl.ds(s * HEAD, HEAD)]
+            put(src, dst, ACT1, (z * ROWS_Y + y_to) * 2 + core, d == 0)
+    expect(ACT1, acts.at[x, core], acts.at[0, 0, pl.ds(0, ROWS_Y - 1)])
 
     for h in range(HEADS):
         strip = pl.ds(h * HEAD, HEAD)
@@ -241,14 +258,6 @@
     arrived(LOAD)
     forward(PICKS)
 
-    for d in range(ROWS_Y):
-        y_to = lax.rem(y + d, ROWS_Y)
-        for s in range(2):
-            src = act_in.at[:, pl.ds(pl.multiple_of((y_to + ROWS_Y * s) * HEAD, HEAD), HEAD)]
-            dst = acts.at[x, core, y, :, pl.ds(s * HEAD, HEAD)]
-            put(src, dst, ACT1, (z * ROWS_Y + y_to) * 2 + core, d == 0)
-    expect(ACT1, acts.at[x, core], acts.at[0, 0, pl.ds(0, ROWS_Y - 1)])
-
     column = lax.broadcasted_iota(jnp.int32, (1, TERMS), 1)
     step_rows = 4 * PIECE
     row = lax.broadcasted_iota(jnp.int32, (step_rows, TERMS), 0)
@@ -287,9 +296,12 @@
         x_from = lax.rem(x + ROWS_X - d, ROWS_X)
         expect(ALONG_X + d, acts.at[x_from, core], acts.at[0, 0])
 
-    for j in range(PICKS):
-        arrived(P2 + j)
-        forward(j)
+    arrived(P2)
+    forward(0)
+    arrived(P2 + 1)
+    forward(1)
+    arrived(P2+2)
+    forward(2)
 
     mine_at = order[chip]
     alive = [selection[j, mine_at] != mine_at for j in range(PICKS)] + [True]
@@ -354,11 +366,6 @@
     remote(dq_give, dq_got, DQ_PART, sibling).start()
     expect(DQ_PART, dq_got, dq_give)
 
-    for d in range(1, ROWS_X):
-        arrived(ALONG_X + d)
-    remote(acts.at[:, core], acts.at[:, core], ACT3, sibling).start()
-    expect(ACT3, acts.at[:, other], acts.at[:, 0])
-
     for j in range(PICKS):
         arrived(BACK2 + j)
         both = [landed[j, :, kind].reshape(TERMS, HEAD) for kind in range(2)]
@@ -380,6 +387,7 @@
             here = dz == 0 and dy == 0
             put(sums.at[target], final.at[chip], BACK1 + group, target * 2 + core, here)
     leaving.append((BACK1 + group, sums.at[pl.ds(0, CHIPS - 1)]))
+    todo.extend(range(4))
 
     arrived(DQ_PART)
     for h in range(HEADS):
@@ -388,15 +396,15 @@
         dq_rows[:, pl.ds(h * HEAD, HEAD)] = dq.T.astype(BF16)
     local(dq_rows, dq_out, DQ).start()
     expect(DQ, dq_out)
-    arrived(ACT3)
-
-    def chunk_of(step):
-        g = lax.rem(z + (0, 1, 3, 2)[step], CHUNKS)
-        return g, pl.ds(pl.multiple_of(g * CHUNK, CHUNK), CHUNK)
+    for d in range(1, ROWS_X):
+        arrived(ALONG_X + d)
+    remote(acts.at[:, core], acts.at[:, core], ACT3, sibling).start()
+    expect(ACT3, acts.at[:, other], acts.at[:, 0])
 
     def collect(step):
         g, rows = chunk_of(step)
         take(final.at[pl.ds(0, 2 * ROWS_Y)], BACK1 + g)
+        todo.remove(step)
         near = final[pl.ds(g * ROWS_Y, ROWS_Y)].astype(F32)
         far = final[pl.ds(CLASSES + g * ROWS_Y, ROWS_Y)].astype(F32)
         both = near + far
@@ -442,10 +450,13 @@
                     def _(src=src, dst=dst):
                         local(src, dst, SUMS).start()
 
-    for step in range(CHUNKS):
-        collect(step)
+    collect(0)
+    collect(1)
+    collect(2)
+    collect(3)
     local(grads, dkv_out, DKV).start()
     expect(DKV, dkv_out)
+    arrived(ACT3)
     for step in range(CHUNKS - 1):
         project(step)
     project(3)

time: 79.3 us -> 66.9 us (0.84)
  Pallas kernels: 78.5 us -> 66.1 us
    pallas_call x1, Pallas kernels: 76.7 us -> 64.3 us  [body(): pl.pallas_call(kernel, out_shape=(jax.ShapeDtypeStruct((HALF, HEADS * HEA...]
where the time goes in v4:
time: 66.9 us; the launch traced here: 66.7 us
  Pallas kernels  66.1 us (99%)
    pallas_call x1, Pallas kernels, body(): pl.pallas_call(kernel, out_shape=(jax.ShapeDtypeStruct((HALF, HEADS * HEA...  64.3 us
    pallas_call x1, Pallas kernels, body(): pl.pallas_call(copy_kernel, out_shape=tuple((jax.ShapeDtypeStruct(s, t) f...  1.76 us

profile of v4, /device:TPU:1, one launch (start us, length us, event | category | flops | bytes accessed | tf_op | source)
XLA Modules:
  0.0 66.7 jit_solution(13003741550744049560)
XLA Ops:
  0.6 64.3 %attention_backward.1 = (bf16[256,512]{1,0:T(8,128)(2,1)}, bf16[2,256,128]{2,1,0:T(8,128)(2,1)}, f32[2,64,128]{2,1,0:T(8,128)}) custom-call(bf16[256,1024]{1,0:T(8,128)(2,1)} %act_in.1, bf16[256,512]{1,0:T(8,128)(2,1)} %q_in.1, bf16[16,16,128]{2,1,0:T(8,128)(2,1)} %bitcast.3, bf16[16,16,128]{2,1,0:T(8,128)(2,1)} %bitcast.4, bf16[256,512]{1,0:T(8,128)(2,1)} %go_in.1, ...), custom_call_target="tpu_custom_call" | custom-call | tf_op jit(solution)/shard_map/attention_backward/pallas_call | solution.py:491
  65.0 1.8 %copy_out.1 = (bf16[256,512]{1,0:T(8,128)(2,1)}, bf16[256,128]{1,0:T(8,128)(2,1)}, bf16[256,128]{1,0:T(8,128)(2,1)}, f32[64,128]{1,0:T(8,128)}, f32[64,128]{1,0:T(8,128)}) custom-call(bf16[256,512]{1,0:T(8,128)(2,1)} %get-tuple-element.8.dq, bf16[2,256,128]{2,1,0:T(8,128)(2,1)} %get-tuple-element.9.dkv, f32[2,64,128]{2,1,0:T(8,128)} %get-tuple-element.10.dw), custom_call_target="tpu_custom_call" | custom-call | tf_op jit(solution)/shard_map/copy_out/pallas_call | solution.py:555

commit v5 on v4

--- a/solution.py
+++ b/solution.py
@@ -32,13 +32,14 @@
 EXP_SCALE = SCALE * math.log2(math.e)
 LOW = -1e30
 
-(LOAD, P1, PACK, ACT1, ACT3, STATS, SUMS, LISTS, ORDER, DQ, DQ_PART, DKV) = range(12)
-P2 = 12
+(LOAD, P1, PACK, ACT1, STATS, SUMS, LISTS, ORDER, DQ, DQ_PART, DKV) = range(11)
+P2 = 11
 ALONG_X = P2 + PICKS
 BACK2 = ALONG_X + ROWS_X
 BACK1 = BACK2 + PICKS
 GATHER = BACK1 + CHUNKS
-SEMS = GATHER + CHUNKS
+ACROSS = GATHER + CHUNKS
+SEMS = ACROSS + ROWS_X
 
 
 def rows_dot(left, right):
@@ -166,17 +167,24 @@
 
     barrier = pltpu.get_barrier_semaphore()
 
-    def greet(d, carry):
+    def hello(ctx, tp=None):
         pl.semaphore_signal(
-            barrier, inc=1, device_id=(lax.rem(c + d, 2 * CHIPS), x), device_id_type=MESH
+            barrier, inc=1, device_id=(ctx, x if tp is None else tp), device_id_type=MESH
         )
-        return carry
-
-    lax.fori_loop(1, 2 * CHIPS, greet, 0)
+
+    far_first = (4, 3, 5, 2, 6, 1, 7, 0)
+    peers = 0
+    for dz in far_first:
+        for dy in (2, 1, 3, 0):
+            if dz or dy:
+                hello(chip_at(dz, dy) * 2 + core)
+                peers += 1
+            if dz == 0 or dy == 0:
+                hello(chip_at(dz, dy) * 2 + other)
+                peers += 1
     for d in range(1, ROWS_X):
-        pl.semaphore_signal(
-            barrier, inc=1, device_id=(c, lax.rem(x + d, ROWS_X)), device_id_type=MESH
-        )
+        hello(c, lax.rem(x + d, ROWS_X))
+        peers += 1
 
     local(selection_in, selection, LISTS).start()
     local(order_in, order, ORDER).start()
@@ -187,9 +195,8 @@
     expect(PACK, packed)
     arrived(PACK)
 
-    pl.semaphore_wait(barrier, 2 * CHIPS - 1 + ROWS_X - 1)
-
-    far_first = (4, 3, 5, 2, 6, 1, 7, 0)
+    pl.semaphore_wait(barrier, peers)
+
     for dz in far_first:
         for dy in (2, 1, 3, 0):
             target = chip_at(dz, dy)
@@ -255,6 +262,30 @@
             stats[j, 1, :, block] = jnp.sum(weights, axis=0, keepdims=True)
             stats[j, 2, :, block] = jnp.sum(weights * gp, axis=0, keepdims=True)
 
+
+    arrived(P1)
+
+    for j in range(PICKS):
+        for n in range(CLASSES):
+            dz, dy = served[n // ROWS_Y], n % ROWS_Y
+            target = chip_at(dz, dy)
+            picked[j, n] = held[table[target, j]]
+            dst = kv.at[j, piece_class]
+            put(picked.at[j, n], dst, P2 + j, target * 2 + core, n == 3 * ROWS_Y)
+        expect(P2 + j, kv.at[j], kv.at[0, pl.ds(0, CLASSES - 1)])
+
+    def across(d):
+        x_from = lax.rem(x + ROWS_X - d, ROWS_X)
+        remote(acts.at[x_from, core], acts.at[x_from, core], ACROSS + d, sibling).start()
+        expect(ACROSS + d, acts.at[x_from, other], acts.at[0, 0])
+
+    arrived(ACT1)
+    for d in (1, 3):
+        x_to = lax.rem(x + d, ROWS_X)
+        remote(acts.at[x, core], acts.at[x, core], ALONG_X + d, c, x_to).start()
+        x_from = lax.rem(x + ROWS_X - d, ROWS_X)
+        expect(ALONG_X + d, acts.at[x_from, core], acts.at[0, 0])
+    across(0)
     arrived(LOAD)
     forward(PICKS)
 
@@ -278,23 +309,6 @@
 
         lax.fori_loop(0, CHIPS // 4, fill, 0)
 
-    arrived(P1)
-
-    for j in range(PICKS):
-        for n in range(CLASSES):
-            dz, dy = served[n // ROWS_Y], n % ROWS_Y
-            target = chip_at(dz, dy)
-            picked[j, n] = held[table[target, j]]
-            dst = kv.at[j, piece_class]
-            put(picked.at[j, n], dst, P2 + j, target * 2 + core, n == 3 * ROWS_Y)
-        expect(P2 + j, kv.at[j], kv.at[0, pl.ds(0, CLASSES - 1)])
-
-    arrived(ACT1)
-    for d in range(1, ROWS_X):
-        x_to = lax.rem(x + d, ROWS_X)
-        remote(acts.at[x, core], acts.at[x, core], ALONG_X + d, c, x_to).start()
-        x_from = lax.rem(x + ROWS_X - d, ROWS_X)
-        expect(ALONG_X + d, acts.at[x_from, core], acts.at[0, 0])
 
     arrived(P2)
     forward(0)
@@ -356,15 +370,15 @@
     for kind, part in enumerate(backward(PICKS)):
         own_terms[kind] = part
 
-    for h in range(HEADS):
-        gs = low[0, :, :, pl.ds(h * BLOCK, BLOCK)].reshape((PICKS + 1) * HALF, BLOCK)
-        dq = plain_dot(key_t[...], gs)
-        at = pl.ds(h * HALF, HALF)
-        first, second = dq[:, :HALF], dq[:, HALF:]
-        dq_mine[:, at] = jnp.where(core == 0, first, second)
-        dq_give[:, at] = jnp.where(core == 0, second, first)
-    remote(dq_give, dq_got, DQ_PART, sibling).start()
-    expect(DQ_PART, dq_got, dq_give)
+    for d, way in ((1, 2), (3, 0)):
+        x_from = lax.rem(x + ROWS_X - d, ROWS_X)
+        x_far = lax.rem(x + 2, ROWS_X)
+        half = pl.ds(0, 2) if d == 1 else pl.ds(2, 2)
+        arrived(ALONG_X + d)
+        passed = acts.at[x_from, core, half]
+        remote(passed, passed, ALONG_X + way, c, lax.rem(x + d, ROWS_X)).start()
+        expect(ALONG_X + way, acts.at[x_far, core, half], acts.at[0, 0, pl.ds(0, 2)])
+        across(d)
 
     for j in range(PICKS):
         arrived(BACK2 + j)
@@ -389,6 +403,15 @@
     leaving.append((BACK1 + group, sums.at[pl.ds(0, CHIPS - 1)]))
     todo.extend(range(4))
 
+    for h in range(HEADS):
+        gs = low[0, :, :, pl.ds(h * BLOCK, BLOCK)].reshape((PICKS + 1) * HALF, BLOCK)
+        dq = plain_dot(key_t[...], gs)
+        at = pl.ds(h * HALF, HALF)
+        first, second = dq[:, :HALF], dq[:, HALF:]
+        dq_mine[:, at] = jnp.where(core == 0, first, second)
+        dq_give[:, at] = jnp.where(core == 0, second, first)
+    remote(dq_give, dq_got, DQ_PART, sibling).start()
+    expect(DQ_PART, dq_got, dq_give)
     arrived(DQ_PART)
     for h in range(HEADS):
         at = pl.ds(h * HALF, HALF)
@@ -396,10 +419,6 @@
         dq_rows[:, pl.ds(h * HEAD, HEAD)] = dq.T.astype(BF16)
     local(dq_rows, dq_out, DQ).start()
     expect(DQ, dq_out)
-    for d in range(1, ROWS_X):
-        arrived(ALONG_X + d)
-    remote(acts.at[:, core], acts.at[:, core], ACT3, sibling).start()
-    expect(ACT3, acts.at[:, other], acts.at[:, 0])
 
     def collect(step):
         g, rows = chunk_of(step)
@@ -456,7 +475,11 @@
     collect(3)
     local(grads, dkv_out, DKV).start()
     expect(DKV, dkv_out)
-    arrived(ACT3)
+    arrived(ALONG_X)
+    arrived(ALONG_X + 2)
+    across(2)
+    for d in range(ROWS_X):
+        arrived(ACROSS + d)
     for step in range(CHUNKS - 1):
         project(step)
     project(3)

time: 66.9 us -> 63.8 us (0.954)
  Pallas kernels: 66.1 us -> 63 us
    pallas_call x1, Pallas kernels: 64.3 us -> 61.2 us  [body(): pl.pallas_call(kernel, out_shape=(jax.ShapeDtypeStruct((HALF, HEADS * HEA...]
where the time goes in v5:
time: 63.8 us; the launch traced here: 63.6 us
  Pallas kernels  63 us (99%)
  between operations  0.64 us (1%)
    pallas_call x1, Pallas kernels, body(): pl.pallas_call(kernel, out_shape=(jax.ShapeDtypeStruct((HALF, HEADS * HEA...  61.2 us
    pallas_call x1, Pallas kernels, body(): pl.pallas_call(copy_kernel, out_shape=tuple((jax.ShapeDtypeStruct(s, t) f...  1.76 us

profile of v5, /device:TPU:1, one launch (start us, length us, event | category | flops | bytes accessed | tf_op | source)
XLA Modules:
  0.0 63.6 jit_solution(13148494616918620148)
XLA Ops:
  0.6 61.2 %attention_backward.1 = (bf16[256,512]{1,0:T(8,128)(2,1)}, bf16[2,256,128]{2,1,0:T(8,128)(2,1)}, f32[2,64,128]{2,1,0:T(8,128)}) custom-call(bf16[256,1024]{1,0:T(8,128)(2,1)} %act_in.1, bf16[256,512]{1,0:T(8,128)(2,1)} %q_in.1, bf16[16,16,128]{2,1,0:T(8,128)(2,1)} %bitcast.3, bf16[16,16,128]{2,1,0:T(8,128)(2,1)} %bitcast.4, bf16[256,512]{1,0:T(8,128)(2,1)} %go_in.1, ...), custom_call_target="tpu_custom_call" | custom-call | tf_op jit(solution)/shard_map/attention_backward/pallas_call | solution.py:514
  61.9 1.8 %copy_out.1 = (bf16[256,512]{1,0:T(8,128)(2,1)}, bf16[256,128]{1,0:T(8,128)(2,1)}, bf16[256,128]{1,0:T(8,128)(2,1)}, f32[64,128]{1,0:T(8,128)}, f32[64,128]{1,0:T(8,128)}) custom-call(bf16[256,512]{1,0:T(8,128)(2,1)} %get-tuple-element.8.dq, bf16[2,256,128]{2,1,0:T(8,128)(2,1)} %get-tuple-element.9.dkv, f32[2,64,128]{2,1,0:T(8,128)} %get-tuple-element.10.dw), custom_call_target="tpu_custom_call" | custom-call | tf_op jit(solution)/shard_map/copy_out/pallas_call | solution.py:578

commit v6 on v5

--- a/solution.py
+++ b/solution.py
@@ -160,6 +160,7 @@
             arrived(sem)
         for sem, ref in leaving:
             sent(ref, sem)
+        leaving.clear()
 
     def chunk_of(step):
         g = lax.rem(z + (0, 1, 3, 2)[step], CHUNKS)
@@ -258,9 +259,9 @@
             gp = rows_dot(values, qd[1, block, :])
             exps[j, :, block] = weights
             gprobs[j, :, block] = gp
-            stats[j, 0, :, block] = top
-            stats[j, 1, :, block] = jnp.sum(weights, axis=0, keepdims=True)
-            stats[j, 2, :, block] = jnp.sum(weights * gp, axis=0, keepdims=True)
+            stats[j, 0, pl.ds(h, 1), :] = top
+            stats[j, 1, pl.ds(h, 1), :] = jnp.sum(weights, axis=0, keepdims=True)
+            stats[j, 2, pl.ds(h, 1), :] = jnp.sum(weights * gp, axis=0, keepdims=True)
 
 
     arrived(P1)
@@ -326,34 +327,34 @@
     peak = stats[PICKS, 0]
     for j in range(PICKS):
         peak = jnp.maximum(peak, jnp.where(alive[j], stats[j, 0], LOW))
-    total = jnp.zeros((1, QUERIES), F32)
-    turned = jnp.zeros((1, QUERIES), F32)
+    total = jnp.zeros((HEADS, BLOCK), F32)
+    turned = jnp.zeros((HEADS, BLOCK), F32)
     parts = []
     for j in range(PICKS + 1):
         part = jnp.where(alive[j], part_of(stats[j, 0], peak), 0.0)
         parts.append(part)
         total = total + part * stats[j, 1]
         turned = turned + part * stats[j, 2]
-    my_stats[pl.ds(0, 1), :] = peak
-    my_stats[pl.ds(1, 1), :] = total
-    my_stats[pl.ds(2, 1), :] = turned
+    my_stats[0] = peak
+    my_stats[1] = total
+    my_stats[2] = turned
     remote(my_stats, their_stats, STATS, sibling).start()
     expect(STATS, their_stats, my_stats)
     arrived(STATS)
-    their_peak = their_stats[pl.ds(0, 1), :]
+    their_peak = their_stats[0]
     top = jnp.maximum(peak, their_peak)
     mine_part = part_of(peak, top)
     their_part = part_of(their_peak, top)
-    share = 1.0 / (mine_part * total + their_part * their_stats[pl.ds(1, 1), :])
-    delta[...] = (mine_part * turned + their_part * their_stats[pl.ds(2, 1), :]) * share
+    share = 1.0 / (mine_part * total + their_part * their_stats[1])
+    delta[...] = (mine_part * turned + their_part * their_stats[2]) * share
     for j in range(PICKS + 1):
         factors[j] = parts[j] * (mine_part * share)
 
     def backward(j):
         for h in range(HEADS):
             block = pl.ds(h * BLOCK, BLOCK)
-            probs = exps[j, :, block] * factors[j, :, block]
-            gs = probs * (gprobs[j, :, block] - delta[:, block])
+            probs = exps[j, :, block] * factors[j, pl.ds(h, 1), :]
+            gs = probs * (gprobs[j, :, block] - delta[pl.ds(h, 1), :])
             low[1, j, :, block] = probs.astype(BF16)
             low[0, j, :, block] = gs.astype(BF16)
         return plain_dot(low[0, j], qd[0]) * SCALE, plain_dot(low[1, j], qd[1])
@@ -483,6 +484,7 @@
     for step in range(CHUNKS - 1):
         project(step)
     project(3)
+    finish()
     expect(SUMS, wide_in, held.at[pl.ds(0, (2 * ROWS_Z - 1) * HEAD // (4 * PIECE))])
     arrived(SUMS)
     for kind in range(2):
@@ -529,11 +531,11 @@
             pltpu.VMEM((HEAD, (PICKS + 1) * HALF), BF16),
             pltpu.VMEM((PICKS + 1, HALF, QUERIES), F32),
             pltpu.VMEM((PICKS + 1, HALF, QUERIES), F32),
-            pltpu.VMEM((PICKS + 1, 3, 1, QUERIES), F32),
-            pltpu.VMEM((8, QUERIES), F32),
-            pltpu.VMEM((8, QUERIES), F32),
-            pltpu.VMEM((PICKS + 1, 1, QUERIES), F32),
-            pltpu.VMEM((1, QUERIES), F32),
+            pltpu.VMEM((PICKS + 1, 3, HEADS, BLOCK), F32),
+            pltpu.VMEM((3, HEADS, BLOCK), F32),
+            pltpu.VMEM((3, HEADS, BLOCK), F32),
+            pltpu.VMEM((PICKS + 1, HEADS, BLOCK), F32),
+            pltpu.VMEM((HEADS, BLOCK), F32),
             pltpu.VMEM((2, PICKS + 1, HALF, QUERIES), BF16),
             pltpu.VMEM((PICKS, CLASSES, 2, PIECE, HEAD), BF16),
             pltpu.VMEM((PICKS, CLASSES, 2, PIECE, HEAD), BF16),

time: 63.8 us -> 63.6 us (level)
  no operation moved by 1% of the time
where the time goes in v6:
time: 63.6 us; the launch traced here: 63.5 us
  Pallas kernels  62.8 us (99%)
  between operations  0.64 us (1%)
    pallas_call x1, Pallas kernels, body(): pl.pallas_call(kernel, out_shape=(jax.ShapeDtypeStruct((HALF, HEADS * HEA...  61.1 us
    pallas_call x1, Pallas kernels, body(): pl.pallas_call(copy_kernel, out_shape=tuple((jax.ShapeDtypeStruct(s, t) f...  1.76 us

profile of v6, /device:TPU:1, one launch (start us, length us, event | category | flops | bytes accessed | tf_op | source)
XLA Modules:
  0.0 63.5 jit_solution(4389194691666566410)
XLA Ops:
  0.6 61.1 %attention_backward.1 = (bf16[256,512]{1,0:T(8,128)(2,1)}, bf16[2,256,128]{2,1,0:T(8,128)(2,1)}, f32[2,64,128]{2,1,0:T(8,128)}) custom-call(bf16[256,1024]{1,0:T(8,128)(2,1)} %act_in.1, bf16[256,512]{1,0:T(8,128)(2,1)} %q_in.1, bf16[16,16,128]{2,1,0:T(8,128)(2,1)} %bitcast.3, bf16[16,16,128]{2,1,0:T(8,128)(2,1)} %bitcast.4, bf16[256,512]{1,0:T(8,128)(2,1)} %go_in.1, ...), custom_call_target="tpu_custom_call" | custom-call | tf_op jit(solution)/shard_map/attention_backward/pallas_call | solution.py:516
  61.7 1.8 %copy_out.1 = (bf16[256,512]{1,0:T(8,128)(2,1)}, bf16[256,128]{1,0:T(8,128)(2,1)}, bf16[256,128]{1,0:T(8,128)(2,1)}, f32[64,128]{1,0:T(8,128)}, f32[64,128]{1,0:T(8,128)}) custom-call(bf16[256,512]{1,0:T(8,128)(2,1)} %get-tuple-element.8.dq, bf16[2,256,128]{2,1,0:T(8,128)(2,1)} %get-tuple-element.9.dkv, f32[2,64,128]{2,1,0:T(8,128)} %get-tuple-element.10.dw), custom_call_target="tpu_custom_call" | custom-call | tf_op jit(solution)/shard_map/copy_out/pallas_call | solution.py:580
